TPU v7x, 512 devices: a whole 4x4x16 slice. The times are simulated.
512 devices in a mesh: pipe: 2 (over core), row: 16 (over z), col: 16 (over y, x).
Axes of the slice: x: 4, y: 4, z: 16, core: 2. Of those that a mesh axis runs over, the one named last changes fastest.
Arguments:
- fwd_in: bfloat16 [2, 512, 6144], P('pipe', 'col', 'row'), may hold values from -6 to 6
- saved_in: bfloat16 [2, 512, 6144], P('pipe', 'col', 'row'), may hold values from -6 to 6
- saved_gate: bfloat16 [2, 512, 14336], P('pipe', 'row', 'col'), may hold values from -6 to 6
- saved_up: bfloat16 [2, 512, 14336], P('pipe', 'row', 'col'), may hold values from -6 to 6
- grad_out: bfloat16 [2, 512, 6144], P('pipe', 'col', 'row'), may hold values from -6 to 6
- w_gate: bfloat16 [2, 6144, 14336], P('pipe', 'row', 'col'), may hold values from -0.109375 to 0.109375
- w_up: bfloat16 [2, 6144, 14336], P('pipe', 'row', 'col'), may hold values from -0.109375 to 0.109375
- w_down: bfloat16 [2, 6144, 14336], P('pipe', 'row', 'col'), may hold values from -0.0625 to 0.0625
- mask_gate: int32 [2, 48, 112], P('pipe', 'row', 'col'), may hold values 0 or 1
- mask_up: int32 [2, 48, 112], P('pipe', 'row', 'col'), may hold values 0 or 1
- mask_down: int32 [2, 48, 112], P('pipe', 'row', 'col'), may hold values 0 or 1
- counts: int32 [2], replicated, may hold values from 256 to 512, as said below
Outputs:
- handoff: bfloat16 [2, 512, 6144], P('pipe', 'col', 'row')
- outward: bfloat16 [2, 512, 6144], P('pipe', 'col', 'row')
- grad_gate: bfloat16 [2, 6144, 14336], P('pipe', 'row', 'col')
- grad_up: bfloat16 [2, 6144, 14336], P('pipe', 'row', 'col')
- grad_down: bfloat16 [2, 6144, 14336], P('pipe', 'row', 'col')
Inputs may be any that keep to these rules, and one draw needn't show every extreme that they name: counts[0] and counts[1] are the numbers of valid leading tokens of the two micro-batches; in every draw one of them equals 512.
All inputs are finite; a program needn't handle non-finite values. No bound on the sum of `mask_gate` or of `mask_up` or of `mask_down` on one device may be relied on, other than what follows from the above.
Results may differ from a plain program's by a relative error of at most 0.035.
Values may be sent and summed in bfloat16 or wider, within the bound.
A program may use at most 64 MiB of HBM per device.

v0:
```python
import jax
import jax.numpy as jnp
from jax import lax
from jax.sharding import PartitionSpec as P

BLOCK = 128


def from_partner(x, axis, distance):
    return lax.ppermute(x, axis, [(i, i ^ 1 << distance) for i in range(lax.axis_size(axis))])


def widen(weight, block_mask, dtype):
    grid_rows, grid_cols = block_mask.shape
    grid = block_mask.astype(dtype)[:, None, :, None]
    shaped = weight.reshape(grid_rows, BLOCK, grid_cols, BLOCK)
    return (shaped * grid).reshape(grid_rows * BLOCK, grid_cols * BLOCK)


def mask_full(block_mask):
    grid_rows, grid_cols = block_mask.shape
    grid = block_mask.astype(jnp.float32)[:, None, :, None]
    return jnp.broadcast_to(grid, (grid_rows, BLOCK, grid_cols, BLOCK)).reshape(
        grid_rows * BLOCK, grid_cols * BLOCK
    )


def times_trans(left, right):
    return lax.dot_general(
        left, right, (((1,), (1,)), ((), ())), preferred_element_type=jnp.float32
    )


def trans_times(left, right):
    return lax.dot_general(
        left, right, (((0,), (0,)), ((), ())), preferred_element_type=jnp.float32
    )


def on_device(
    fwd_in,
    saved_in,
    saved_gate,
    saved_up,
    grad_out,
    w_gate,
    w_up,
    w_down,
    mask_gate,
    mask_up,
    mask_down,
    counts,
):
    inputs = fwd_in[0]
    tok_local = inputs.shape[0]
    positions = lax.axis_index("col") * tok_local + jnp.arange(tok_local, dtype=jnp.int32)
    cotangent = jnp.where(positions[:, None] < counts[1], grad_out[0], jnp.zeros_like(grad_out[0]))
    inputs_all, cot_all, stored_all = (
        lax.all_gather(inputs, "col", axis=0, tiled=True),
        lax.all_gather(cotangent, "col", axis=0, tiled=True),
        lax.all_gather(saved_in[0], "col", axis=0, tiled=True),
    )
    gate_eff = widen(w_gate[0], mask_gate[0], jnp.bfloat16)
    up_eff = widen(w_up[0], mask_up[0], jnp.bfloat16)
    down_eff = widen(w_down[0], mask_down[0], jnp.bfloat16)
    part_gate = jnp.dot(inputs_all, gate_eff, preferred_element_type=jnp.float32)
    part_up = jnp.dot(inputs_all, up_eff, preferred_element_type=jnp.float32)
    part_dhid = jnp.dot(cot_all, down_eff, preferred_element_type=jnp.float32)
    gate_f, up_f, dhid = (
        lax.psum_scatter(
            part_gate.astype(jnp.bfloat16), "row", scatter_dimension=0, tiled=True
        ).astype(jnp.float32),
        lax.psum_scatter(
            part_up.astype(jnp.bfloat16), "row", scatter_dimension=0, tiled=True
        ).astype(jnp.float32),
        lax.psum_scatter(
            part_dhid.astype(jnp.bfloat16), "row", scatter_dimension=0, tiled=True
        ).astype(jnp.float32),
    )
    gate_b = saved_gate[0].astype(jnp.float32)
    up_b = saved_up[0].astype(jnp.float32)
    hidden_f = (gate_f * jax.nn.sigmoid(gate_f) * up_f).astype(jnp.bfloat16)
    sigma = jax.nn.sigmoid(gate_b)
    dgate = (dhid * up_b * sigma * (1.0 + gate_b * (1.0 - sigma))).astype(jnp.bfloat16)
    grad_upv = (dhid * gate_b * sigma).astype(jnp.bfloat16)
    hidden_b = (gate_b * sigma * up_b).astype(jnp.bfloat16)
    hidden_fa, dgate_all, dup_all, hidden_ba = (
        lax.all_gather(hidden_f, "row", axis=0, tiled=True),
        lax.all_gather(dgate, "row", axis=0, tiled=True),
        lax.all_gather(grad_upv, "row", axis=0, tiled=True),
        lax.all_gather(hidden_b, "row", axis=0, tiled=True),
    )
    part_out = times_trans(hidden_fa, down_eff)
    part_back = times_trans(dgate_all, gate_eff) + times_trans(dup_all, up_eff)
    ffn_f, back_sum = (
        lax.psum_scatter(
            part_out.astype(jnp.bfloat16), "col", scatter_dimension=0, tiled=True
        ).astype(jnp.float32),
        lax.psum_scatter(
            part_back.astype(jnp.bfloat16), "col", scatter_dimension=0, tiled=True
        ).astype(jnp.float32),
    )
    output = jnp.where(
        positions[:, None] < counts[0], inputs.astype(jnp.float32) + ffn_f, 0.0
    ).astype(jnp.bfloat16)
    input_grad = (cotangent.astype(jnp.float32) + back_sum).astype(jnp.bfloat16)
    grad_gatev = (mask_full(mask_gate[0]) * trans_times(stored_all, dgate_all)).astype(jnp.bfloat16)
    grad_upw = (mask_full(mask_up[0]) * trans_times(stored_all, dup_all)).astype(jnp.bfloat16)
    grad_downv = (mask_full(mask_down[0]) * trans_times(cot_all, hidden_ba)).astype(jnp.bfloat16)
    first_section = lax.axis_index("pipe") == 0
    message = jnp.where(first_section, output, input_grad)
    received = from_partner(message, "pipe", 0)
    leaving = jnp.where(first_section, input_grad, output)
    return (received[None], leaving[None], grad_gatev[None], grad_upw[None], grad_downv[None])


def solution(mesh):
    in_specs = (
        P("pipe", "col", "row"),
        P("pipe", "col", "row"),
        P("pipe", "row", "col"),
        P("pipe", "row", "col"),
        P("pipe", "col", "row"),
        P("pipe", "row", "col"),
        P("pipe", "row", "col"),
        P("pipe", "row", "col"),
        P("pipe", "row", "col"),
        P("pipe", "row", "col"),
        P("pipe", "row", "col"),
        P(),
    )
    out_specs = (
        P("pipe", "col", "row"),
        P("pipe", "col", "row"),
        P("pipe", "row", "col"),
        P("pipe", "row", "col"),
        P("pipe", "row", "col"),
    )
    return jax.shard_map(
        on_device, mesh=mesh, in_specs=in_specs, out_specs=out_specs, check_vma=False
    )
```

profile of v0, /device:TPU:1, one launch (start us, length us, event | category | flops | bytes accessed | tf_op | source)
XLA Modules:
  0.0 448.0 jit_solution(6454707411354366389)
XLA Ops:
  7.2 0.0 reduce-scatter.16.cloned.1.call-start
  7.2 0.8 fusion.37
  8.0 19.8 %all-gather = bf16[1,512,384]{2,1,0:T(8,128)(2,1)S(1)} all-gather(bf16[1,32,384]{2,1,0:T(8,128)(2,1)} %param.12), channel_id=2, replica_groups=mesh['pipe'=2,'row'=16,'col'=16] {'col'}, dimensions={1}, use_global_device_ids=true | all-gather | bytes 417792 | tf_op jit(solution)/shard_map/all_gather | solution.py:59
  27.8 0.2 mul.76
  28.0 1.8 fusion.5
  29.8 0.0 copy-start.19
  29.8 0.0 copy-start.10
  29.8 1.3 copy.50
  31.1 0.0 reduce-scatter.16.cloned.1.call-update
  31.1 0.0 reduce-scatter.18.cloned.1.call-start
  31.2 0.2 mul.80
  31.4 0.9 copy-done.4
  32.3 0.7 fusion.6
  33.0 0.0 copy-start.20
  33.0 0.0 copy-start.18
  33.0 1.3 copy.52
  34.3 0.0 reduce-scatter.18.cloned.1.call-update
  34.3 0.0 reduce-scatter.20.cloned.1.call-start
  34.4 0.6 fusion.38
  35.0 0.7 fusion.33
  35.7 0.1 bitcast_select_fusion
  35.8 17.7 %all_gather.23 = bf16[512,384]{1,0:T(8,128)(2,1)S(1)} all-gather(bf16[32,384]{1,0:T(8,128)(2,1)S(1)} %bitcast_select_fusion), channel_id=1, replica_groups=mesh['pipe'=2,'row'=16,'col'=16] {'col'}, dimensions={0}, use_global_device_ids=true | all-gather | bytes 417792 | tf_op jit(solution)/shard_map/all_gather | solution.py:60
  53.5 0.2 mul.84
  53.7 0.6 copy-done.2
  54.3 0.3 copy-done.6
  54.6 1.6 convolution_convert_fusion
  56.2 0.0 reduce-scatter.20.cloned.1.call-update
  56.3 0.0 reduce-scatter.12.cloned.1.call-start
  56.3 0.2 broadcast_in_dim.69
  56.5 0.3 copy.90
  56.8 0.4 copy.47
  57.2 0.2 broadcast_in_dim.67
  57.4 0.3 copy.91
  57.7 1.6 copy.46
  59.3 19.6 %all-gather.1 = bf16[1,512,384]{2,1,0:T(8,128)(2,1)} all-gather(bf16[1,32,384]{2,1,0:T(8,128)(2,1)} %param.13), channel_id=3, replica_groups=mesh['pipe'=2,'row'=16,'col'=16] {'col'}, dimensions={1}, use_global_device_ids=true | all-gather | bytes 417792 | tf_op jit(solution)/shard_map/all_gather | solution.py:61
  78.9 0.7 fusion.34
  79.6 19.2 %reduce-scatter.16.cloned.1.call-done = bf16[32,896]{1,0:T(8,128)(2,1)} async-done(((bf16[512,896]{1,0:T(8,128)(2,1)}), bf16[32,896]{1,0:T(8,128)(2,1)}) %reduce-scatter.16.cloned.1.call-update) | async-done | bytes 57360 | tf_op jit(solution)/shard_map/reduce_scatter | solution.py:70
  98.8 71.0 %reduce-scatter.18.cloned.1.call-done = bf16[32,896]{1,0:T(8,128)(2,1)} async-done(((bf16[512,896]{1,0:T(8,128)(2,1)}), bf16[32,896]{1,0:T(8,128)(2,1)}) %reduce-scatter.18.cloned.1.call-update) | async-done | bytes 57360 | tf_op jit(solution)/shard_map/reduce_scatter | solution.py:73
  169.8 0.9 fusion.30
  170.7 26.9 %all_gather.22 = bf16[512,896]{1,0:T(8,128)(2,1)S(1)} all-gather(bf16[32,896]{1,0:T(8,128)(2,1)S(1)} %fusion.30), channel_id=1, replica_groups=mesh['pipe'=2,'row'=16,'col'=16] {'row'}, dimensions={0}, use_global_device_ids=true | all-gather | bytes 974848 | tf_op jit(solution)/shard_map/all_gather | solution.py:88
  197.6 2.5 convolution_convert_fusion.3
  200.2 0.0 reduce-scatter.12.cloned.1.call-update
  200.2 0.0 reduce-scatter.14.cloned.1.call-start
  200.3 39.6 %reduce-scatter.20.cloned.1.call-done = bf16[32,896]{1,0:T(8,128)(2,1)} async-done(((bf16[512,896]{1,0:T(8,128)(2,1)}), bf16[32,896]{1,0:T(8,128)(2,1)}) %reduce-scatter.20.cloned.1.call-update) | async-done | bytes 57360 | tf_op jit(solution)/shard_map/reduce_scatter | solution.py:76
  239.9 1.5 fusion.23
  241.4 27.5 %all_gather.24 = bf16[512,896]{1,0:T(8,128)(2,1)S(1)} all-gather(bf16[32,896]{1,0:T(8,128)(2,1)S(1)} %get-tuple-element.26), channel_id=1, replica_groups=mesh['pipe'=2,'row'=16,'col'=16] {'row'}, dimensions={0}, use_global_device_ids=true | all-gather | bytes 974848 | tf_op jit(solution)/shard_map/all_gather | solution.py:89
  268.9 1.9 fusion.15
  270.9 26.3 %all_gather.25 = bf16[512,896]{1,0:T(8,128)(2,1)S(1)} all-gather(bf16[32,896]{1,0:T(8,128)(2,1)S(1)} %get-tuple-element.27), channel_id=1, replica_groups=mesh['pipe'=2,'row'=16,'col'=16] {'row'}, dimensions={0}, use_global_device_ids=true | all-gather | bytes 974848 | tf_op jit(solution)/shard_map/all_gather | solution.py:90
  297.2 1.4 fusion.10
  298.6 0.0 reduce-scatter.14.cloned.1.call-update
  298.6 2.6 fusion.8
  301.3 0.0 copy-start.15
  301.3 0.7 fusion.9
  302.0 0.1 copy-done.12
  302.1 26.6 %all_gather.27 = bf16[512,896]{1,0:T(8,128)(2,1)S(1)} all-gather(bf16[32,896]{1,0:T(8,128)(2,1)S(1)} %copy-done.12), channel_id=1, replica_groups=mesh['pipe'=2,'row'=16,'col'=16] {'row'}, dimensions={0}, use_global_device_ids=true | all-gather | bytes 974848 | tf_op jit(solution)/shard_map/all_gather | solution.py:91
  328.7 11.0 %reduce-scatter.12.cloned.1.call-done = bf16[32,384]{1,0:T(8,128)(2,1)} async-done(((bf16[512,384]{1,0:T(8,128)(2,1)}), bf16[32,384]{1,0:T(8,128)(2,1)}) %reduce-scatter.12.cloned.1.call-update) | async-done | bytes 24592 | tf_op jit(solution)/shard_map/reduce_scatter | solution.py:96
  339.7 91.6 %reduce-scatter.14.cloned.1.call-done = bf16[32,384]{1,0:T(8,128)(2,1)} async-done(((bf16[512,384]{1,0:T(8,128)(2,1)}), bf16[32,384]{1,0:T(8,128)(2,1)}) %reduce-scatter.14.cloned.1.call-update) | async-done | bytes 24592 | tf_op jit(solution)/shard_map/reduce_scatter | solution.py:99
  431.3 1.4 select_bitcast_fusion
  432.7 4.2 collective-permute-start
  436.9 0.2 broadcast_in_dim.71
  437.1 1.5 fusion.7
  438.6 1.1 copy.49
  439.8 1.1 copy.48
  440.9 0.6 copy.99
  (42 shorter events, 0.1 us)
Async XLA Ops:
  7.2 91.6 %reduce-scatter.16.cloned.1.call-start = ((), (), s32[]{:S(2)}) async-start(), calls=%async_computation.7 | async-start | bytes 974848 | tf_op jit(solution)/shard_map/reduce_scatter | solution.py:70
  29.8 1.4 copy-start.19
  29.8 2.5 copy-start.10
  31.1 138.7 %reduce-scatter.18.cloned.1.call-start = ((), (), s32[]{:S(2)}) async-start(), calls=%async_computation.8 | async-start | bytes 974848 | tf_op jit(solution)/shard_map/reduce_scatter | solution.py:73
  31.4 0.9 copy-start.4
  33.0 1.4 copy-start.20
  33.0 1.4 copy-start.18
  33.0 2.7 copy-start.14
  34.3 20.3 %copy-start.9 = (bf16[1,384,896]{2,1,0:T(8,128)(2,1)S(1)}, bf16[1,384,896]{2,1,0:T(8,128)(2,1)}, u32[]{:S(2)}) copy-start(bf16[1,384,896]{2,1,0:T(8,128)(2,1)} %param.19) | copy-start | bytes 2064388
  34.3 205.6 %reduce-scatter.20.cloned.1.call-start = ((), (), s32[]{:S(2)}) async-start(), calls=%async_computation.9 | async-start | bytes 974848 | tf_op jit(solution)/shard_map/reduce_scatter | solution.py:76
  53.5 0.8 copy-start.2
  53.7 0.9 copy-start.6
  56.3 283.4 %reduce-scatter.12.cloned.1.call-start = ((), (), s32[]{:S(2)}) async-start(), calls=%async_computation.5 | async-start | bytes 417792 | tf_op jit(solution)/shard_map/reduce_scatter | solution.py:96
  59.3 138.4 %copy-start.7 = (bf16[3,128,7,128]{3,2,1,0:T(8,128)(2,1)S(1)}, bf16[3,128,7,128]{3,2,1,0:T(8,128)(2,1)}, u32[]{:S(2)}) copy-start(bf16[3,128,7,128]{3,2,1,0:T(8,128)(2,1)} %copy-done.6) | copy-start | bytes 2064388
  197.6 42.3 %copy-start.16 = (bf16[1,32,896]{2,1,0:T(8,128)(2,1)S(1)}, bf16[1,32,896]{2,1,0:T(8,128)(2,1)}, u32[]{:S(2)}) copy-start(bf16[1,32,896]{2,1,0:T(8,128)(2,1)} %param.15) | copy-start | bytes 172036
  197.6 42.3 %copy-start.17 = (bf16[1,32,896]{2,1,0:T(8,128)(2,1)S(1)}, bf16[1,32,896]{2,1,0:T(8,128)(2,1)}, u32[]{:S(2)}) copy-start(bf16[1,32,896]{2,1,0:T(8,128)(2,1)} %param.14) | copy-start | bytes 172036
  200.2 231.0 %reduce-scatter.14.cloned.1.call-start = ((), (), s32[]{:S(2)}) async-start(), calls=%async_computation.6 | async-start | bytes 417792 | tf_op jit(solution)/shard_map/reduce_scatter | solution.py:99
  268.9 28.2 %copy-start.5 = (bf16[3,128,7,128]{3,2,1,0:T(8,128)(2,1)S(1)}, bf16[3,128,7,128]{3,2,1,0:T(8,128)(2,1)}, u32[]{:S(2)}) copy-start(bf16[3,128,7,128]{3,2,1,0:T(8,128)(2,1)} %copy-done.4) | copy-start | bytes 2064388
  268.9 28.2 %copy-start.11 = (bf16[1,384,896]{2,1,0:T(8,128)(2,1)S(1)}, bf16[1,384,896]{2,1,0:T(8,128)(2,1)}, u32[]{:S(2)}) copy-start(bf16[1,384,896]{2,1,0:T(8,128)(2,1)} %param.18) | copy-start | bytes 2064388
  298.6 2.7 copy-start
  298.6 2.7 copy-start.1
  301.3 0.8 copy-start.12
  301.3 130.0 %copy-start.13 = (bf16[1,32,384]{2,1,0:T(8,128)(2,1)S(1)}, bf16[1,32,384]{2,1,0:T(8,128)(2,1)}, u32[]{:S(2)}) copy-start(bf16[1,32,384]{2,1,0:T(8,128)(2,1)} %param.12) | copy-start | bytes 73732
  301.3 130.0 %copy-start.15 = (bf16[1,32,384]{2,1,0:T(8,128)(2,1)S(1)}, bf16[1,32,384]{2,1,0:T(8,128)(2,1)}, u32[]{:S(2)}) copy-start(bf16[1,32,384]{2,1,0:T(8,128)(2,1)} %param.16) | copy-start | bytes 73732
  302.0 135.1 %copy-start.3 = (bf16[512,384]{1,0:T(8,128)(2,1)S(1)}, bf16[512,384]{1,0:T(8,128)(2,1)}, u32[]{:S(2)}) copy-start(bf16[512,384]{1,0:T(8,128)(2,1)} %copy-done.2) | copy-start | bytes 1179652
  432.7 8.2 %collective-permute-start = (bf16[32,384]{1,0:T(8,128)(2,1)S(1)}, bf16[32,384]{1,0:T(8,128)(2,1)S(1)}, u32[]{:S(2)}, u32[]{:S(2)}) collective-permute-start(bf16[32,384]{1,0:T(8,128)(2,1)S(1)} %get-tuple-element.29), channel_id=1, source_target_pairs={{0,256},{256,0},{1,257},{257,1},{2,258},{258,2},{3,259},{259,3},{4... | collective-permute-start | bytes 73736 | tf_op jit(solution)/shard_map/ppermute | solution.py:10
  437.1 1.5 copy-start.8
Sparse Core Ops, SparseCore 0:
  31.3 67.5 reduce-scatter.15
  101.8 67.9 reduce-scatter.17
  172.6 67.2 reduce-scatter.19
  244.9 94.7 reduce-scatter.11
  344.2 87.0 reduce-scatter.13
where the time goes:
time: 449 us; the launch traced here: 448 us
  waiting for transfers between devices  232 us (52%)
  blocking collectives  165 us (37%)
  matrix products  14.8 us (3%)
  between operations  14.1 us (3%)
  local copies, waits for them, and re-layouts  11.6 us (3%)
  other arithmetic  6.03 us (1%)
    reduce_scatter x1, waiting for transfers between devices, on_device(): lax.psum_scatter(part_back.astype(jnp.bfloat16), 'col', scatter_dimension...  91.6 us
    reduce_scatter x1, waiting for transfers between devices, on_device(): lax.psum_scatter(part_up.astype(jnp.bfloat16), 'row', scatter_dimension=0...  71 us
    reduce_scatter x1, waiting for transfers between devices, on_device(): lax.psum_scatter(part_dhid.astype(jnp.bfloat16), 'row', scatter_dimension...  39.6 us
    all_gather x1, blocking collectives, on_device(): lax.all_gather(dgate, 'row', axis=0, tiled=True)  27.5 us
    all_gather x1, blocking collectives, on_device(): lax.all_gather(hidden_f, 'row', axis=0, tiled=True)  26.9 us
    all_gather x1, blocking collectives, on_device(): lax.all_gather(hidden_b, 'row', axis=0, tiled=True)  26.6 us
    all_gather x1, blocking collectives, on_device(): lax.all_gather(grad_upv, 'row', axis=0, tiled=True)  26.3 us
    all_gather x1, blocking collectives, on_device(): lax.all_gather(inputs, 'col', axis=0, tiled=True)  19.8 us
  transfers between devices with their start and end apart: 6, of which 5 were waited for; matrix products, arithmetic and copies ran while one was open for 5% of the time, Pallas kernels for 0%

commit v1 on v0

v1 whole, which is shorter than its diff:
```python
import functools

import jax
import jax.numpy as jnp
from jax import lax
from jax.experimental import pallas as pl
from jax.experimental.pallas import tpu as pltpu
from jax.sharding import PartitionSpec as P

BLOCK = 128
BF16 = jnp.bfloat16
F32 = jnp.float32
MESH = pl.DeviceIdType.MESH
GATE, UP, DHID, HF, DG, DU, HB = range(7)


def kernel(
    dims,
    fwd_in, saved_in, saved_gate, saved_up, grad_out,
    w_gate, w_up, w_down,
    mask_gate, mask_up, mask_down, counts,
    handoff, outward, grad_gate, grad_up, grad_down,
    fx, ct, sv, go_v, sg_v, su_v, wg_v, wu_v, wd_v,
    part, land_a, land_b, full,
    out_y, out_dx, fold_y, fold_dx, mid_y, mid_dx, tail_y, tail_dx,
    message, leaving, received, stage,
    load_sem, z_send, z_recv, g1_send, g1_recv, g2_send, g2_recv,
    p_send, p_recv, store_sem,
):
    ring, ny, nx, chunk, depth, width = dims
    half = ring // 2
    row = lax.axis_index("row")
    col = lax.axis_index("col")
    pipe = lax.axis_index("pipe")
    y, x = col // nx, lax.rem(col, nx)

    loads = [
        pltpu.make_async_copy(grad_out.at[0], go_v, load_sem.at[0]),
        pltpu.make_async_copy(saved_gate.at[0], sg_v, load_sem.at[1]),
        pltpu.make_async_copy(saved_up.at[0], su_v, load_sem.at[2]),
        pltpu.make_async_copy(fwd_in.at[0], fx.at[y, x], load_sem.at[3]),
        pltpu.make_async_copy(saved_in.at[0], sv.at[y, x], load_sem.at[4]),
        pltpu.make_async_copy(w_gate.at[0], wg_v, load_sem.at[5]),
        pltpu.make_async_copy(w_up.at[0], wu_v, load_sem.at[6]),
        pltpu.make_async_copy(w_down.at[0], wd_v, load_sem.at[7]),
    ]
    for load in loads:
        load.start()

    right, left = lax.rem(row + 1, ring), lax.rem(row + ring - 1, ring)
    barrier = pltpu.get_barrier_semaphore()
    peers = [{"row": right}, {"row": left}, {"pipe": 1 - pipe}]
    peers += [{"col": y * nx + lax.rem(x + d, nx)} for d in range(1, nx)]
    peers += [{"col": lax.rem(y + d, ny) * nx + x} for d in range(1, ny)]
    for peer in peers:
        pl.semaphore_signal(barrier, inc=1, device_id=peer, device_id_type=MESH)

    loads[0].wait()
    positions = col * chunk + lax.broadcasted_iota(jnp.int32, (chunk, depth), 0)
    ct[x, y] = jnp.where(positions < counts[1], go_v[...].astype(F32), 0.0).astype(BF16)
    loads[1].wait()
    loads[2].wait()
    gate_b, up_b = sg_v[...].astype(F32), su_v[...].astype(F32)
    full[HB - HF, 0] = (gate_b * jax.nn.sigmoid(gate_b) * up_b).astype(BF16)
    loads[3].wait()
    loads[4].wait()

    pl.semaphore_wait(barrier, len(peers))

    sends = []

    def remote(src, dst, send_sem, recv_sem, device):
        return pltpu.make_async_remote_copy(
            src_ref=src, dst_ref=dst, send_sem=send_sem, recv_sem=recv_sem,
            device_id=device, device_id_type=MESH,
        )

    def launch(copy):
        copy.start()
        sends.append(copy)

    def arms(unit):
        longer = 1 if unit % 2 == 0 else -1
        return ((longer, half), (-longer, half - 1))

    def z_copy(unit, arm, step):
        d, n = arms(unit)[arm]
        if unit <= DHID:
            src = part.at[unit, (d * (n - step)) % ring]
            dst = (land_a if arm == 0 else land_b).at[unit, step]
        else:
            src = full.at[unit - HF, (-d * step) % ring]
            dst = full.at[unit - HF, (-d * (step + 1)) % ring]
        return remote(
            src, dst, z_send.at[unit, arm, step], z_recv.at[unit, arm, step],
            {"row": right if d == 1 else left},
        )

    def z_step(unit, step):
        for arm in range(2):
            d, n = arms(unit)[arm]
            if step > 0 and step <= n:
                z_copy(unit, arm, step - 1).wait_recv()
                if unit <= DHID and step < n:
                    slot = (d * (n - step)) % ring
                    land = (land_a if arm == 0 else land_b)[unit, step - 1]
                    part[unit, slot] = (part[unit, slot].astype(F32) + land.astype(F32)).astype(BF16)
            if step < n:
                launch(z_copy(unit, arm, step))

    def reduced(unit):
        return (
            part[unit, 0].astype(F32)
            + land_a[unit, half - 1].astype(F32)
            + land_b[unit, half - 2].astype(F32)
        )

    def where_xy(a, b):
        return {"col": a * nx + b}

    def where_yx(a, b):
        return {"col": b * nx + a}

    def gather_copy(which, phase, d):
        buf, a, b, na, nb, where = (
            (fx, y, x, ny, nx, where_xy), (ct, x, y, nx, ny, where_yx), (sv, y, x, ny, nx, where_xy)
        )[which]
        if phase == 1:
            ref, device = buf.at[a, b], where(a, lax.rem(b + d, nb))
            return remote(ref, ref, g1_send.at[which, d - 1], g1_recv.at[which, d - 1], device)
        ref, device = buf.at[a], where(lax.rem(a + d, na), b)
        return remote(ref, ref, g2_send.at[which, d - 1], g2_recv.at[which, d - 1], device)

    def gather_start(which, phase):
        for d in range(1, nx):
            launch(gather_copy(which, phase, d))

    def gather_wait(which, phase):
        for d in range(1, nx):
            gather_copy(which, phase, d).wait_recv()

    def fold_copy(which, phase, d):
        buf, land, mid, tail, a, b, na, nb, where = (
            (out_y, fold_y, mid_y, tail_y, y, x, ny, nx, where_xy),
            (out_dx, fold_dx, mid_dx, tail_dx, x, y, nx, ny, where_yx),
        )[which]
        if phase == 1:
            other = lax.rem(a + d, na)
            return remote(
                buf.at[other], land.at[d - 1],
                g1_send.at[3 + which, d - 1], g1_recv.at[3 + which, d - 1], where(other, b),
            )
        other = lax.rem(b + d, nb)
        return remote(
            mid.at[other], tail.at[d - 1],
            g2_send.at[3 + which, d - 1], g2_recv.at[3 + which, d - 1], where(a, other),
        )

    def fold_start(which):
        for d in range(1, nx):
            launch(fold_copy(which, 1, d))

    def fold_middle(which):
        buf, land, mid, a = ((out_y, fold_y, mid_y, y), (out_dx, fold_dx, mid_dx, x))[which]
        for d in range(1, nx):
            fold_copy(which, 1, d).wait_recv()
        for k in range(nx):
            total = buf[a, k].astype(F32)
            for d in range(1, nx):
                total += land[d - 1, k].astype(F32)
            mid[k] = total.astype(BF16)
        for d in range(1, nx):
            launch(fold_copy(which, 2, d))

    def fold_end(which):
        mid, tail, b = ((mid_y, tail_y, x), (mid_dx, tail_dx, y))[which]
        total = mid[b].astype(F32)
        for d in range(1, nx):
            fold_copy(which, 2, d).wait_recv()
            total += tail[d - 1].astype(F32)
        return total

    def apply_mask(weight, mask):
        for i in range(depth // BLOCK):
            for k in range(width // BLOCK):
                at = (pl.ds(i * BLOCK, BLOCK), pl.ds(k * BLOCK, BLOCK))
                weight[at] = (weight[at].astype(F32) * mask[0, i, k].astype(F32)).astype(BF16)

    def place(which, j):
        t = lax.rem(row + j, ring)
        return (t // nx, lax.rem(t, nx)) if which != 1 else (lax.rem(t, nx), t // nx)

    group = min(4, ring)

    def rows_of(which, buf, start, count):
        return jnp.concatenate([buf[place(which, start + k)] for k in range(count)], axis=0)

    def partials(which, buf, targets):
        for start in range(0, ring, group):
            lhs = rows_of(which, buf, start, group)
            for unit, weight in targets:
                product = jnp.dot(lhs, weight[...], preferred_element_type=F32).astype(BF16)
                part[unit, pl.ds(start, group)] = product.reshape(group, chunk, width)

    def back_product(which, buf, pairs):
        for start in range(0, ring, group):
            total = None
            for unit, weight in pairs:
                lhs = full[unit - HF, pl.ds(start, group)].reshape(group * chunk, width)
                term = lax.dot_general(
                    lhs, weight[...], (((1,), (1,)), ((), ())), preferred_element_type=F32
                )
                total = term if total is None else total + term
            total = total.astype(BF16)
            for k in range(group):
                buf[place(which, start + k)] = total[k * chunk:(k + 1) * chunk]

    def weight_grad(which, buf, unit, mask, index, out):
        lhs = rows_of(which, buf, 0, ring)
        for k in range(0, width, BLOCK):
            rhs = full[unit - HF, :, :, pl.ds(k, BLOCK)].reshape(ring * chunk, BLOCK)
            product = lax.dot_general(
                lhs, rhs, (((0,), (0,)), ((), ())), preferred_element_type=F32
            )
            for i in range(depth // BLOCK):
                rows = pl.ds(i * BLOCK, BLOCK)
                stage[index, rows, pl.ds(k, BLOCK)] = (
                    product[i * BLOCK:(i + 1) * BLOCK] * mask[0, i, k // BLOCK].astype(F32)
                ).astype(BF16)
        store = pltpu.make_async_copy(stage.at[index], out.at[0], store_sem.at[index])
        store.start()
        return store

    stores = []

    z_step(HB, 0)
    gather_start(0, 1)
    gather_start(1, 1)
    loads[5].wait()
    apply_mask(wg_v, mask_gate)
    loads[6].wait()
    apply_mask(wu_v, mask_up)
    z_step(HB, 1)
    gather_wait(0, 1)
    gather_start(0, 2)
    gather_wait(1, 1)
    gather_start(1, 2)
    loads[7].wait()
    apply_mask(wd_v, mask_down)
    z_step(HB, 2)
    gather_wait(0, 2)
    partials(0, fx, [(GATE, wg_v), (UP, wu_v)])
    z_step(GATE, 0)
    z_step(UP, 0)
    gather_wait(1, 2)
    gather_start(2, 1)
    partials(1, ct, [(DHID, wd_v)])
    z_step(DHID, 0)
    for s in range(1, half + 1):
        z_step(GATE, s)
        z_step(UP, s)
        z_step(DHID, s)
        if s == 2:
            gather_wait(2, 1)
            gather_start(2, 2)
    gate_f, up_f = reduced(GATE), reduced(UP)
    full[0, 0] = (gate_f * jax.nn.sigmoid(gate_f) * up_f).astype(BF16)
    z_step(HF, 0)
    dhid = reduced(DHID)
    gate_b, up_b = sg_v[...].astype(F32), su_v[...].astype(F32)
    sig = jax.nn.sigmoid(gate_b)
    full[DG - HF, 0] = (dhid * up_b * sig * (1.0 + gate_b * (1.0 - sig))).astype(BF16)
    full[DU - HF, 0] = (dhid * gate_b * sig).astype(BF16)
    z_step(DG, 0)
    z_step(DU, 0)
    for s in range(1, half + 1):
        z_step(HF, s)
        z_step(DG, s)
        z_step(DU, s)
    back_product(0, out_y, [(HF, wd_v)])
    fold_start(0)
    back_product(1, out_dx, [(DG, wg_v), (DU, wu_v)])
    fold_start(1)
    z_step(HB, 3)
    gather_wait(2, 2)
    stores.append(weight_grad(2, sv, DG, mask_gate, 0, grad_gate))
    z_step(HB, 4)
    fold_middle(0)
    fold_middle(1)
    stores.append(weight_grad(2, sv, DU, mask_up, 1, grad_up))
    z_step(HB, 5)
    ffn = fold_end(0)
    result_y = jnp.where(positions < counts[0], fx[y, x].astype(F32) + ffn, 0.0).astype(BF16)
    result_dx = (ct[x, y].astype(F32) + fold_end(1)).astype(BF16)
    first = jnp.full((chunk, depth), pipe, jnp.int32) == 0
    message[...] = jnp.where(first, result_y.astype(F32), result_dx.astype(F32)).astype(BF16)
    leaving[...] = jnp.where(first, result_dx.astype(F32), result_y.astype(F32)).astype(BF16)
    swap = remote(message, received, p_send, p_recv, {"pipe": 1 - pipe})
    launch(swap)
    stores.append(pltpu.make_async_copy(leaving, outward.at[0], store_sem.at[3]))
    stores[-1].start()
    for s in range(6, half + 1):
        z_step(HB, s)
    swap.wait_recv()
    stores.append(pltpu.make_async_copy(received, handoff.at[0], store_sem.at[4]))
    stores[-1].start()
    stores.append(weight_grad(1, ct, HB, mask_down, 2, grad_down))
    for copy in sends:
        copy.wait_send()
    for store in stores:
        store.wait()


def on_device(nx, *args):
    fwd_in, saved_gate = args[0], args[2]
    _, chunk, depth = fwd_in.shape
    _, chunk_r, width = saved_gate.shape
    cols = lax.axis_size("col")
    ring = lax.axis_size("row")
    ny = cols // nx
    assert chunk == chunk_r and ring == cols and ny == nx
    half = ring // 2
    dims = (ring, ny, nx, chunk, depth, width)
    wide = (chunk, width)
    slim = (chunk, depth)
    any_spec = pl.BlockSpec(memory_space=pl.ANY)
    smem_spec = pl.BlockSpec(memory_space=pltpu.SMEM)
    weight = jax.ShapeDtypeStruct((1, depth, width), BF16)
    act = jax.ShapeDtypeStruct((1, chunk, depth), BF16)
    dma = pltpu.SemaphoreType.DMA
    return pl.pallas_call(
        functools.partial(kernel, dims),
        out_shape=(act, act, weight, weight, weight),
        in_specs=[any_spec] * 8 + [smem_spec] * 4,
        out_specs=(any_spec,) * 5,
        scratch_shapes=[
            pltpu.VMEM((ny, nx) + slim, BF16),
            pltpu.VMEM((nx, ny) + slim, BF16),
            pltpu.VMEM((ny, nx) + slim, BF16),
            pltpu.VMEM(slim, BF16),
            pltpu.VMEM(wide, BF16),
            pltpu.VMEM(wide, BF16),
            pltpu.VMEM((depth, width), BF16),
            pltpu.VMEM((depth, width), BF16),
            pltpu.VMEM((depth, width), BF16),
            pltpu.VMEM((3, ring) + wide, BF16),
            pltpu.VMEM((3, half) + wide, BF16),
            pltpu.VMEM((3, max(half - 1, 1)) + wide, BF16),
            pltpu.VMEM((4, ring) + wide, BF16),
            pltpu.VMEM((ny, nx) + slim, BF16),
            pltpu.VMEM((nx, ny) + slim, BF16),
            pltpu.VMEM((ny - 1, nx) + slim, BF16),
            pltpu.VMEM((nx - 1, ny) + slim, BF16),
            pltpu.VMEM((nx,) + slim, BF16),
            pltpu.VMEM((ny,) + slim, BF16),
            pltpu.VMEM((nx - 1,) + slim, BF16),
            pltpu.VMEM((ny - 1,) + slim, BF16),
            pltpu.VMEM(slim, BF16),
            pltpu.VMEM(slim, BF16),
            pltpu.VMEM(slim, BF16),
            pltpu.VMEM((3, depth, width), BF16),
            dma((8,)),
            dma((7, 2, half)),
            dma((7, 2, half)),
            dma((5, nx - 1)),
            dma((5, nx - 1)),
            dma((5, nx - 1)),
            dma((5, nx - 1)),
            dma,
            dma,
            dma((5,)),
        ],
        compiler_params=pltpu.CompilerParams(
            collective_id=0, has_side_effects=True, vmem_limit_bytes=48 * 1024 * 1024
        ),
    )(*args)


def solution(mesh):
    nx = 1
    while nx * nx < mesh.shape["col"]:
        nx += 1
    tokens = P("pipe", "col", "row")
    grid = P("pipe", "row", "col")
    in_specs = (tokens, tokens, grid, grid, tokens) + (grid,) * 6 + (P(),)
    out_specs = (tokens, tokens, grid, grid, grid)
    return jax.shard_map(
        functools.partial(on_device, nx), mesh=mesh, in_specs=in_specs, out_specs=out_specs, check_vma=False
    )
```

time: 449 us -> 130 us (0.29)
  the two profiles are of different devices: /device:TPU:1 before, /device:TPU:2 now
where the time goes in v1:
time: 130 us; the launch traced here: 129 us
  Pallas kernels  115 us (88%)
  local copies, waits for them, and re-layouts  12.9 us (10%)
    pallas_call x1, Pallas kernels, on_device(): pl.pallas_call(functools.partial(kernel, dims), out_shape=(act, act, weig...  115 us
    unnamed x30, local copies, waits for them, and re-layouts  12.9 us

profile of v1, /device:TPU:2, one launch (start us, length us, event | category | flops | bytes accessed | tf_op | source)
XLA Modules:
  0.0 129.0 jit_solution(9916802446012019069)
XLA Ops:
  0.6 0.0 copy-start.9
  0.6 0.7 copy.17.mask_gate
  1.3 0.0 copy-done.9
  1.3 0.0 copy-start.10
  1.3 0.7 copy-done.10
  2.0 0.0 copy-start.8
  2.0 0.7 copy-done.8
  2.7 0.0 copy-start
  2.7 1.1 copy-done
  3.8 0.0 copy-start.1
  3.8 1.1 copy-done.1
  4.9 0.0 copy-start.2
  4.9 1.1 copy-done.2
  6.0 0.0 copy-start.3
  6.0 0.8 copy-done.3
  6.8 0.0 copy-start.4
  6.8 0.8 copy-done.4
  7.6 0.0 copy-start.5
  7.6 0.7 copy-done.5
  8.3 0.0 copy-start.6
  8.3 0.7 copy-done.6
  9.1 0.0 copy-start.7
  9.1 0.7 copy-done.7
  9.8 115.4 %shard_map.155 = (bf16[1,32,384]{2,1,0:T(8,128)(2,1)S(1)}, bf16[1,32,384]{2,1,0:T(8,128)(2,1)S(1)}, bf16[1,384,896]{2,1,0:T(8,128)(2,1)S(1)}, bf16[1,384,896]{2,1,0:T(8,128)(2,1)S(1)}, bf16[1,384,896]{2,1,0:T(8,128)(2,1)S(1)}) custom-call(bf16[1,32,384]{2,1,0:T(8,128)(2,1)S(1)} %copy-done.5, bf16[1,32,384]{2,1,0:T(8,128)(2,1)S(1)} %copy-done.6, ...), custom_call_target="tpu_custom_call" | custom-call | tf_op jit(solution)/shard_map/pallas_call | solution.py:331
  125.2 0.6 copy.25
  125.9 0.6 copy.26
  126.5 0.8 copy.27
  127.3 0.8 copy.28
  128.2 0.8 copy.29
  (2 shorter events, 0.0 us)
Async XLA Ops:
  0.6 0.7 copy-start.9
  1.3 0.7 copy-start.10
  2.0 0.7 copy-start.8
  2.7 1.1 copy-start
  3.8 1.1 copy-start.1
  4.9 1.1 copy-start.2
  6.0 0.8 copy-start.3
  6.8 0.8 copy-start.4
  7.6 0.7 copy-start.5
  8.3 0.7 copy-start.6
  9.1 0.7 copy-start.7

commit v2 on v1

v2 whole, which is shorter than its diff:
```python
import functools

import jax
import jax.numpy as jnp
from jax import lax
from jax.experimental import pallas as pl
from jax.experimental.pallas import tpu as pltpu
from jax.sharding import PartitionSpec as P

BLOCK = 128
BF16 = jnp.bfloat16
F32 = jnp.float32
MESH = pl.DeviceIdType.MESH
GATE, UP, DHID, HF, DG, DU, HB = range(7)
IN_X, IN_COT, IN_SAVED = range(3)
OUT_Y, OUT_DX = range(2)


def kernel(
    dims,
    fwd_in, saved_in, saved_gate, saved_up, grad_out,
    w_gate, w_up, w_down,
    mask_gate, mask_up, mask_down, counts,
    handoff, outward, grad_gate, grad_up, grad_down,
    acts, go_v, sg_v, su_v, weights, mask_v, mask_rows,
    part, land_a, land_b, full, turned,
    outs, out_land, message, leaving, stage,
    load_sem, z_send, z_recv, g_send, g_recv, f_send, f_recv,
    p_send, p_recv, store_sem,
):
    ring, chunk, depth, width = dims
    half = ring // 2
    row = lax.axis_index("row")
    col = lax.axis_index("col")
    pipe = lax.axis_index("pipe")

    masks = (mask_gate, mask_up, mask_down)
    moves = [
        (fwd_in.at[0], acts.at[IN_X, col]),
        (grad_out.at[0], go_v),
        (saved_gate.at[0], sg_v),
        (saved_up.at[0], su_v),
        (saved_in.at[0], acts.at[IN_SAVED, col]),
    ]
    moves += [(mask, mask_v.at[k]) for k, mask in enumerate(masks)]
    moves += [(w.at[0], weights.at[k]) for k, w in enumerate((w_gate, w_up, w_down))]
    loads = [pltpu.make_async_copy(src, dst, load_sem.at[k]) for k, (src, dst) in enumerate(moves)]
    for load in loads:
        load.start()

    right, left = lax.rem(row + 1, ring), lax.rem(row + ring - 1, ring)
    barrier = pltpu.get_barrier_semaphore()
    peers = [{"row": right}, {"row": left}, {"pipe": 1 - pipe}]
    peers += [{"col": lax.rem(col + d, ring)} for d in range(1, ring)]
    for peer in peers:
        pl.semaphore_signal(barrier, inc=1, device_id=peer, device_id_type=MESH)

    loads[1].wait()
    positions = col * chunk + lax.broadcasted_iota(jnp.int32, (chunk, depth), 0)
    acts[IN_COT, col] = jnp.where(positions < counts[1], go_v[...].astype(F32), 0.0).astype(BF16)
    loads[2].wait()
    loads[3].wait()
    gate_b, up_b = sg_v[...].astype(F32), su_v[...].astype(F32)
    full[HB - HF, 0] = (gate_b * jax.nn.sigmoid(gate_b) * up_b).astype(BF16)
    loads[0].wait()
    loads[4].wait()

    pl.semaphore_wait(barrier, len(peers))

    sends = []

    def remote(src, dst, send_sem, recv_sem, device):
        return pltpu.make_async_remote_copy(
            src_ref=src, dst_ref=dst, send_sem=send_sem, recv_sem=recv_sem,
            device_id=device, device_id_type=MESH,
        )

    def launch(copy):
        copy.start()
        sends.append(copy)

    def arms(unit):
        longer = 1 if unit % 2 == 0 else -1
        return ((longer, half), (-longer, half - 1))

    def z_copy(unit, arm, step):
        d, n = arms(unit)[arm]
        if unit <= DHID:
            src = part.at[unit, (d * (n - step)) % ring]
            dst = (land_a if arm == 0 else land_b).at[unit, step]
        else:
            src = full.at[unit - HF, (-d * step) % ring]
            dst = full.at[unit - HF, (-d * (step + 1)) % ring]
        return remote(
            src, dst, z_send.at[unit, arm, step], z_recv.at[unit, arm, step],
            {"row": right if d == 1 else left},
        )

    def z_step(unit, step):
        for arm in range(2):
            d, n = arms(unit)[arm]
            if step > 0 and step <= n:
                z_copy(unit, arm, step - 1).wait_recv()
                if unit <= DHID and step < n:
                    slot = (d * (n - step)) % ring
                    land = (land_a if arm == 0 else land_b)[unit, step - 1]
                    part[unit, slot] = (part[unit, slot].astype(F32) + land.astype(F32)).astype(BF16)
            if 0 <= step < n:
                launch(z_copy(unit, arm, step))

    def reduced(unit):
        return (
            part[unit, 0].astype(F32)
            + land_a[unit, half - 1].astype(F32)
            + land_b[unit, half - 2].astype(F32)
        )

    def gather_copy(which, d, source, target):
        ref = acts.at[which, source]
        return remote(ref, ref, g_send.at[which, d - 1], g_recv.at[which, d - 1], {"col": target})

    def gather_start(which):
        for d in range(1, ring):
            launch(gather_copy(which, d, col, lax.rem(col + d, ring)))

    def gather_wait(which):
        for d in range(1, ring):
            gather_copy(which, d, lax.rem(col + ring - d, ring), col).wait_recv()

    def fold_copy(which, j):
        owner = lax.rem(row + j, ring)
        d = lax.rem(col - owner + ring, ring)
        index = lax.max(d - 1, 0)
        return owner, remote(
            outs.at[which, j], out_land.at[which, index],
            f_send.at[which, j], f_recv.at[which, index], {"col": owner},
        )

    def fold_start(which, j):
        owner, copy = fold_copy(which, j)

        @pl.when(owner != col)
        def _():
            copy.start()

    def fold_finish(which):
        for j in range(ring):
            owner, copy = fold_copy(which, j)

            @pl.when(owner != col)
            def _():
                copy.wait_send()

    def fold_end(which):
        total = outs[which, lax.rem(col - row + ring, ring)].astype(F32)
        for d in range(1, ring):
            remote(
                outs.at[which, 0], out_land.at[which, d - 1],
                f_send.at[which, 0], f_recv.at[which, d - 1], {"col": lax.rem(col + d, ring)},
            ).wait_recv()
            total += out_land[which, d - 1].astype(F32)
        return total

    def expand_mask(k):
        for i in range(depth // BLOCK):
            row_mask = [
                jnp.broadcast_to(mask_v[k, i, :, b:b + 1].astype(F32), (1, BLOCK))
                for b in range(width // BLOCK)
            ]
            mask_rows[k, i:i + 1, :] = jnp.concatenate(row_mask, axis=1)

    def mask_row(k, i):
        return mask_rows[k, i:i + 1, :]

    def apply_mask(k):
        for i in range(depth // BLOCK):
            at = pl.ds(i * BLOCK, BLOCK)
            weights[k, at] = (weights[k, at].astype(F32) * mask_row(k, i)).astype(BF16)

    def rows_of(which, slots):
        return jnp.concatenate([acts[which, lax.rem(row + j, ring)] for j in slots], axis=0)

    quarter = ring // 4
    first_slots = [(half - quarter // 2 + k) % ring for k in range(quarter)]
    groups = [[(j + g * quarter) % ring for j in first_slots] for g in (0, 3, 1, 2)]

    def partials(which, slots, units):
        lhs = rows_of(which, slots)
        for unit in units:
            product = jnp.dot(lhs, weights[unit], preferred_element_type=F32).astype(BF16)
            for k, j in enumerate(slots):
                part[unit, j] = product[k * chunk:(k + 1) * chunk]

    def back_product(which, slots):
        total = None
        for unit, k in (((HF, 2),), ((DG, 0), (DU, 1)))[which]:
            lhs = jnp.concatenate([full[unit - HF, j] for j in slots], axis=0)
            term = lax.dot_general(
                lhs, weights[k], (((1,), (1,)), ((), ())), preferred_element_type=F32
            )
            total = term if total is None else total + term
        total = total.astype(BF16)
        for k, j in enumerate(slots):
            outs[which, j] = total[k * chunk:(k + 1) * chunk]
            fold_start(which, j)

    def turn(k, which, slots):
        turned[k, :, pl.ds(slots[0] * chunk, len(slots) * chunk)] = rows_of(which, slots).T

    def weight_grad(k, unit, index, out):
        rhs = full[unit - HF].reshape(ring * chunk, width)
        for i in range(depth // BLOCK):
            at = pl.ds(i * BLOCK, BLOCK)
            product = jnp.dot(turned[k, at], rhs, preferred_element_type=F32)
            stage[index, at] = (product * mask_row(index, i)).astype(BF16)
        store = pltpu.make_async_copy(stage.at[index], out.at[0], store_sem.at[index])
        store.start()
        stores.append(store)

    stores = []

    gather_start(IN_X)
    z_step(HB, 0)
    gather_start(IN_COT)
    for k in range(3):
        loads[5 + k].wait()
        expand_mask(k)
    for k in range(2):
        loads[8 + k].wait()
        apply_mask(k)
    z_step(HB, 1)
    loads[10].wait()
    apply_mask(2)
    gather_wait(IN_X)
    partials(IN_X, groups[0], (GATE, UP))
    z_step(GATE, 0)
    z_step(UP, 0)
    for slots in groups[1:]:
        partials(IN_X, slots, (GATE, UP))
    z_step(HB, 2)
    gather_wait(IN_COT)
    partials(IN_COT, groups[0], (DHID,))
    z_step(DHID, 0)
    for slots in groups[1:]:
        partials(IN_COT, slots, (DHID,))
    gather_start(IN_SAVED)
    for s in range(1, half + 1):
        z_step(GATE, s)
        z_step(UP, s)
        if s < half:
            z_step(DHID, s)
        if s == 1:
            z_step(HB, 3)
        if s == 2:
            for g in range(0, ring, quarter):
                turn(0, IN_COT, range(g, g + quarter))
        if s == min(3, half):
            gather_wait(IN_SAVED)
            for g in range(0, ring, quarter):
                turn(1, IN_SAVED, range(g, g + quarter))
    gate_f, up_f = reduced(GATE), reduced(UP)
    full[0, 0] = (gate_f * jax.nn.sigmoid(gate_f) * up_f).astype(BF16)
    z_step(HF, 0)
    z_step(DHID, half)
    dhid = reduced(DHID)
    gate_b, up_b = sg_v[...].astype(F32), su_v[...].astype(F32)
    sig = jax.nn.sigmoid(gate_b)
    full[DG - HF, 0] = (dhid * up_b * sig * (1.0 + gate_b * (1.0 - sig))).astype(BF16)
    full[DU - HF, 0] = (dhid * gate_b * sig).astype(BF16)
    z_step(DG, 0)
    z_step(DU, 0)
    z_step(HB, 4)
    pending = [0]
    for s in range(1, half + 1):
        z_step(HF, s)
        z_step(DG, s)
        z_step(DU, s)
        pending += [s, ring - s] if s < half else [s]
        if s % 2 == 0 or s >= half - 1:
            back_product(OUT_Y, pending)
            back_product(OUT_DX, pending)
            pending = []
    z_step(HB, 5)
    weight_grad(1, DG, 0, grad_gate)
    z_step(HB, 6)
    ffn = fold_end(OUT_Y)
    back = fold_end(OUT_DX)
    result_y = jnp.where(positions < counts[0], acts[IN_X, col].astype(F32) + ffn, 0.0).astype(BF16)
    result_dx = (acts[IN_COT, col].astype(F32) + back).astype(BF16)
    first = jnp.full((chunk, depth), pipe, jnp.int32) == 0
    message[...] = jnp.where(first, result_y.astype(F32), result_dx.astype(F32)).astype(BF16)
    leaving[...] = jnp.where(first, result_dx.astype(F32), result_y.astype(F32)).astype(BF16)
    swap = remote(message, handoff.at[0], p_send, p_recv, {"pipe": 1 - pipe})
    launch(swap)
    stores.append(pltpu.make_async_copy(leaving, outward.at[0], store_sem.at[3]))
    stores[-1].start()
    z_step(HB, 7)
    weight_grad(1, DU, 1, grad_up)
    z_step(HB, 8)
    weight_grad(0, HB, 2, grad_down)
    swap.wait_recv()
    for copy in sends:
        copy.wait_send()
    fold_finish(OUT_Y)
    fold_finish(OUT_DX)
    for store in stores:
        store.wait()


def on_device(*args):
    fwd_in, saved_gate = args[0], args[2]
    _, chunk, depth = fwd_in.shape
    _, chunk_r, width = saved_gate.shape
    ring = lax.axis_size("row")
    assert chunk == chunk_r and ring == lax.axis_size("col")
    half = ring // 2
    dims = (ring, chunk, depth, width)
    wide = (chunk, width)
    slim = (chunk, depth)
    blocks = (depth // BLOCK, width // BLOCK)
    hbm_spec = pl.BlockSpec(memory_space=pltpu.HBM)
    smem_spec = pl.BlockSpec(memory_space=pltpu.SMEM)
    weight = jax.ShapeDtypeStruct((1, depth, width), BF16)
    act = jax.ShapeDtypeStruct((1, chunk, depth), BF16)
    dma = pltpu.SemaphoreType.DMA
    return pl.pallas_call(
        functools.partial(kernel, dims),
        out_shape=(act, act, weight, weight, weight),
        in_specs=[hbm_spec] * 11 + [smem_spec],
        out_specs=(hbm_spec,) * 5,
        scratch_shapes=[
            pltpu.VMEM((3, ring) + slim, BF16),
            pltpu.VMEM(slim, BF16),
            pltpu.VMEM(wide, BF16),
            pltpu.VMEM(wide, BF16),
            pltpu.VMEM((3, depth, width), BF16),
            pltpu.VMEM((3, blocks[0], 1, blocks[1]), jnp.int32),
            pltpu.VMEM((3, 8, width), F32),
            pltpu.VMEM((3, ring) + wide, BF16),
            pltpu.VMEM((3, half) + wide, BF16),
            pltpu.VMEM((3, max(half - 1, 1)) + wide, BF16),
            pltpu.VMEM((4, ring) + wide, BF16),
            pltpu.VMEM((2, depth, ring * chunk), BF16),
            pltpu.VMEM((2, ring) + slim, BF16),
            pltpu.VMEM((2, ring - 1) + slim, BF16),
            pltpu.VMEM(slim, BF16),
            pltpu.VMEM(slim, BF16),
            pltpu.VMEM((3, depth, width), BF16),
            dma((11,)),
            dma((7, 2, half)),
            dma((7, 2, half)),
            dma((3, ring - 1)),
            dma((3, ring - 1)),
            dma((2, ring)),
            dma((2, ring - 1)),
            dma,
            dma,
            dma((4,)),
        ],
        compiler_params=pltpu.CompilerParams(
            collective_id=0, has_side_effects=True, vmem_limit_bytes=63 * 1024 * 1024
        ),
    )(*args[:8], *(jnp.transpose(mask, (1, 0, 2)) for mask in args[8:11]), args[11])


def solution(mesh):
    tokens = P("pipe", "col", "row")
    grid = P("pipe", "row", "col")
    in_specs = (tokens, tokens, grid, grid, tokens) + (grid,) * 6 + (P(),)
    out_specs = (tokens, tokens, grid, grid, grid)
    return jax.shard_map(on_device, mesh=mesh, in_specs=in_specs, out_specs=out_specs, check_vma=False)
```

time: 130 us -> 116 us (0.89)
  Pallas kernels: 115 us -> 108 us
  local copies, waits for them, and re-layouts: 12.9 us -> 6.23 us
    pallas_call x1, Pallas kernels: 115 us -> 108 us  [on_device(): pl.pallas_call(functools.partial(kernel, dims), out_shape=(act, act, weig...]
    unnamed x30 -> x11, local copies, waits for them, and re-layouts: 12.9 us -> 6.23 us
where the time goes in v2:
time: 116 us; the launch traced here: 115 us
  Pallas kernels  108 us (93%)
  local copies, waits for them, and re-layouts  6.23 us (5%)
    pallas_call x1, Pallas kernels, on_device(): pl.pallas_call(functools.partial(kernel, dims), out_shape=(act, act, weig...  108 us
    unnamed x11, local copies, waits for them, and re-layouts  6.23 us

profile of v2, /device:TPU:2, one launch (start us, length us, event | category | flops | bytes accessed | tf_op | source)
XLA Modules:
  0.0 115.3 jit_solution(8162027247192237043)
XLA Ops:
  0.6 108.4 %shard_map.155 = (bf16[1,32,384]{2,1,0:T(8,128)(2,1)}, bf16[1,32,384]{2,1,0:T(8,128)(2,1)}, bf16[1,384,896]{2,1,0:T(8,128)(2,1)}, bf16[1,384,896]{2,1,0:T(8,128)(2,1)}, bf16[1,384,896]{2,1,0:T(8,128)(2,1)}) custom-call(bf16[1,32,384]{2,1,0:T(8,128)(2,1)} %fwd_in.1, bf16[1,32,384]{2,1,0:T(8,128)(2,1)} %saved_in.1, bf16[1,32,896]{2,1,0:T(8,128)(2,1)} %saved_gate.1, ...), custom_call_target="tpu_custom_call" | custom-call | tf_op jit(solution)/shard_map/pallas_call | solution.py:326
  109.1 0.0 copy-start.2
  109.1 1.4 %copy.22 = bf16[1,32,384]{2,1,0:T(8,128)(2,1)} copy(bf16[1,32,384]{2,1,0:T(8,128)(2,1)} %get-tuple-element.10) | data formatting | bytes 49152
  110.4 0.0 copy-done.2
  110.4 0.6 copy.23
  111.0 0.0 copy-start.1
  111.0 2.1 %copy.24 = bf16[1,384,896]{2,1,0:T(8,128)(2,1)} copy(bf16[1,384,896]{2,1,0:T(8,128)(2,1)} %get-tuple-element.12) | data formatting | bytes 1376256
  113.1 0.0 copy-done.1
  113.1 0.0 copy-start
  113.1 0.8 copy.25
  114.0 0.5 copy-done
  114.5 0.8 copy.26
Async XLA Ops:
  109.1 1.4 %copy-start.2 = (bf16[1,32,384]{2,1,0:T(8,128)(2,1)S(1)}, bf16[1,32,384]{2,1,0:T(8,128)(2,1)}, u32[]{:S(2)}) copy-start(bf16[1,32,384]{2,1,0:T(8,128)(2,1)} %get-tuple-element.11) | copy-start | bytes 73732
  111.0 2.1 %copy-start.1 = (bf16[1,384,896]{2,1,0:T(8,128)(2,1)S(1)}, bf16[1,384,896]{2,1,0:T(8,128)(2,1)}, u32[]{:S(2)}) copy-start(bf16[1,384,896]{2,1,0:T(8,128)(2,1)} %get-tuple-element.13) | copy-start | bytes 2064388
  113.1 1.3 %copy-start = (bf16[1,384,896]{2,1,0:T(8,128)(2,1)S(1)}, bf16[1,384,896]{2,1,0:T(8,128)(2,1)}, u32[]{:S(2)}) copy-start(bf16[1,384,896]{2,1,0:T(8,128)(2,1)} %get-tuple-element.14) | copy-start | bytes 2064388

commit v3 on v2

v3 whole, which is shorter than its diff:
```python
import functools

import jax
import jax.numpy as jnp
from jax import lax
from jax.experimental import pallas as pl
from jax.experimental.pallas import tpu as pltpu
from jax.sharding import PartitionSpec as P

BLOCK = 128
BF16 = jnp.bfloat16
F32 = jnp.float32
MESH = pl.DeviceIdType.MESH
VMEM_LIMIT = 63 * 1024 * 1024
GU, DH, HF, DD, HB = range(5)
IN_X, IN_COT, IN_SAVED = range(3)
OUT_Y, OUT_DX = range(2)


def kernel(
    dims,
    fwd_in, saved_in, saved_gate, saved_up, grad_out,
    w_gate, w_up, w_down,
    mask_gate, mask_up, mask_down, counts,
    handoff, outward, grad_gate, grad_up, grad_down,
    acts, go_v, sg_v, su_v, weights, mask_v, mask_rows,
    part_gu, part_dh, full_hf, full_dd, full_hb,
    land_gu_a, land_gu_b, land_dh_a, land_dh_b, turned,
    outs, out_land, message, leaving, stage,
    load_sem, z_send, z_recv, g_send, g_recv, f_send, f_recv,
    p_send, p_recv, store_sem,
):
    ring, nx, chunk, depth, width = dims
    half = ring // 2
    row = lax.axis_index("row")
    col = lax.axis_index("col")
    pipe = lax.axis_index("pipe")
    y, x = col // nx, lax.rem(col, nx)
    right, left = lax.rem(row + 1, ring), lax.rem(row + ring - 1, ring)

    def along_x(d):
        return {"col": y * nx + lax.rem(x + d, nx)}

    def along_y(d):
        return {"col": lax.rem(y + d, nx) * nx + x}

    barrier = pltpu.get_barrier_semaphore()
    peers = [{"row": right}, {"row": left}, {"pipe": 1 - pipe}]
    peers += [along_x(d) for d in range(1, nx)] + [along_y(d) for d in range(1, nx)]
    for peer in peers:
        pl.semaphore_signal(barrier, inc=1, device_id=peer, device_id_type=MESH)

    masks = (mask_gate, mask_up, mask_down)
    moves = [
        (saved_gate.at[0], sg_v),
        (saved_up.at[0], su_v),
        (grad_out.at[0], go_v),
        (fwd_in.at[0], acts.at[IN_X, y, x]),
        (saved_in.at[0], acts.at[IN_SAVED, y, x]),
    ]
    moves += [(mask, mask_v.at[k]) for k, mask in enumerate(masks)]
    moves += [(w.at[0], weights.at[k]) for k, w in enumerate((w_gate, w_up, w_down))]
    loads = [pltpu.make_async_copy(src, dst, load_sem.at[k]) for k, (src, dst) in enumerate(moves)]
    for load in loads:
        load.start()

    pl.semaphore_wait(barrier, len(peers))

    def remote(src, dst, send_sem, recv_sem, device):
        return pltpu.make_async_remote_copy(
            src_ref=src, dst_ref=dst, send_sem=send_sem, recv_sem=recv_sem,
            device_id=device, device_id_type=MESH,
        )

    sums = {GU: (part_gu, land_gu_a, land_gu_b), DH: (part_dh, land_dh_a, land_dh_b)}
    fulls = {HF: full_hf, DD: full_dd, HB: full_hb}

    def arms(stream):
        longer = 1 if stream in (GU, DD) else -1
        return ((longer, half), (-longer, half - 1))

    def z_copy(stream, arm, step):
        d, n = arms(stream)[arm]
        if stream in sums:
            src = sums[stream][0].at[(d * (n - step)) % ring]
            dst = sums[stream][1 + arm].at[step]
        else:
            src = fulls[stream].at[(-d * step) % ring]
            dst = fulls[stream].at[(-d * (step + 1)) % ring]
        return remote(
            src, dst, z_send.at[stream], z_recv.at[stream, arm, step],
            {"row": right if d == 1 else left},
        )

    def z_step(stream, step):
        for arm in range(2):
            d, n = arms(stream)[arm]
            if 0 < step <= n:
                z_copy(stream, arm, step - 1).wait_recv()
                if stream in sums and step < n:
                    part = sums[stream][0]
                    slot = (d * (n - step)) % ring
                    land = sums[stream][1 + arm][step - 1]
                    part[slot] = (part[slot].astype(F32) + land.astype(F32)).astype(BF16)
            if step < n:
                z_copy(stream, arm, step).start()

    def z_finish(stream):
        ref = (sums[stream][0] if stream in sums else fulls[stream]).at[pl.ds(0, ring - 1)]
        remote(ref, ref, z_send.at[stream], z_recv.at[stream, 0, 0], {"row": right}).wait_send()

    def reduced(stream):
        part, land_a, land_b = sums[stream]
        return (
            part[0].astype(F32) + land_a[half - 1].astype(F32) + land_b[half - 2].astype(F32)
        )

    cut = chunk // 2
    halves = (pl.ds(0, cut), pl.ds(cut, cut))

    def gather_start(which, phase, source=None):
        buf = acts.at[which]
        for d in range(1, nx):
            for h, rows in enumerate(halves):
                if phase == 0:
                    dst = buf.at[y, x, rows]
                    src = dst if source is None else source.at[rows]
                    device = along_x(d) if h == 0 else along_y(d)
                else:
                    src = dst = buf.at[y, :, rows] if h == 0 else buf.at[:, x, rows]
                    device = along_y(d) if h == 0 else along_x(d)
                remote(src, dst, g_send.at[which], g_recv.at[which, phase], device).start()

    def gather_wait(which, phase):
        buf = acts.at[which]
        ref = buf.at[0, pl.ds(0, nx - 1)] if phase == 0 else buf.at[pl.ds(0, nx - 1)]
        remote(ref, ref, g_send.at[which], g_recv.at[which, phase], along_x(1)).wait_recv()

    def fold_start(which, j):
        owner = lax.rem(row + j, ring)
        index = lax.max(lax.rem(col - owner + ring, ring) - 1, 0)

        @pl.when(owner != col)
        def _():
            remote(
                outs.at[which, j], out_land.at[which, index],
                f_send.at[which], f_recv.at[which], {"col": owner},
            ).start()

    def fold_all(which):
        return remote(
            outs.at[which, pl.ds(0, ring - 1)], out_land.at[which],
            f_send.at[which], f_recv.at[which], along_x(1),
        )

    def fold_end(which):
        fold_all(which).wait_recv()
        total = outs[which, lax.rem(col - row + ring, ring)].astype(F32)
        for d in range(1, ring):
            total += out_land[which, d - 1].astype(F32)
        return total

    def expand_mask(k):
        for i in range(depth // BLOCK):
            row_mask = [
                jnp.broadcast_to(mask_v[k, i, :, b:b + 1].astype(F32), (1, BLOCK))
                for b in range(width // BLOCK)
            ]
            mask_rows[k, i:i + 1, :] = jnp.concatenate(row_mask, axis=1)

    def mask_row(k, i):
        return mask_rows[k, i:i + 1, :]

    def apply_mask(k):
        loads[5 + k].wait()
        expand_mask(k)
        loads[8 + k].wait()
        for i in range(depth // BLOCK):
            at = pl.ds(i * BLOCK, BLOCK)
            weights[k, at] = (weights[k, at].astype(F32) * mask_row(k, i)).astype(BF16)

    def rows_of(which, slots):
        chunks = [lax.rem(row + j, ring) for j in slots]
        return jnp.concatenate([acts[which, t // nx, lax.rem(t, nx)] for t in chunks], axis=0)

    quarter = ring // 4
    first_slots = [(half - quarter // 2 + k) % ring for k in range(quarter)]
    groups = [[(j + g * quarter) % ring for j in first_slots] for g in (0, 3, 1, 2)]

    def partials(which, slots, part, ks):
        lhs = rows_of(which, slots)
        for u, k in enumerate(ks):
            product = jnp.dot(lhs, weights[k], preferred_element_type=F32).astype(BF16)
            for m, j in enumerate(slots):
                part[j, u] = product[m * chunk:(m + 1) * chunk]

    def back_product(which, slots):
        total = None
        for full, u, k in (((full_hf, 0, 2),), ((full_dd, 0, 0), (full_dd, 1, 1)))[which]:
            lhs = jnp.concatenate([full[j, u] for j in slots], axis=0)
            term = lax.dot_general(
                lhs, weights[k], (((1,), (1,)), ((), ())), preferred_element_type=F32
            )
            total = term if total is None else total + term
        total = total.astype(BF16)
        for m, j in enumerate(slots):
            outs[which, j] = total[m * chunk:(m + 1) * chunk]
            fold_start(which, j)

    def turn(k, which):
        for g in range(0, ring, quarter):
            slots = range(g, g + quarter)
            turned[k, :, pl.ds(g * chunk, quarter * chunk)] = rows_of(which, slots).T

    stores = []

    def weight_grad(k, full, u, index, out):
        rhs = full[:, u].reshape(ring * chunk, width)
        for i in range(depth // BLOCK):
            at = pl.ds(i * BLOCK, BLOCK)
            product = jnp.dot(turned[k, at], rhs, preferred_element_type=F32)
            stage[index, at] = (product * mask_row(index, i)).astype(BF16)
        store = pltpu.make_async_copy(stage.at[index], out.at[0], store_sem.at[index])
        store.start()
        stores.append(store)

    gather_start(IN_X, 0, fwd_in.at[0])
    loads[0].wait()
    loads[1].wait()
    gate_b, up_b = sg_v[...].astype(F32), su_v[...].astype(F32)
    full_hb[0, 0] = (gate_b * jax.nn.sigmoid(gate_b) * up_b).astype(BF16)
    z_step(HB, 0)
    loads[2].wait()
    positions = col * chunk + lax.broadcasted_iota(jnp.int32, (chunk, depth), 0)
    acts[IN_COT, y, x] = jnp.where(positions < counts[1], go_v[...].astype(F32), 0.0).astype(BF16)
    gather_start(IN_COT, 0)
    loads[3].wait()
    apply_mask(0)
    gather_wait(IN_X, 0)
    gather_start(IN_X, 1)
    z_step(HB, 1)
    gather_wait(IN_COT, 0)
    gather_start(IN_COT, 1)
    apply_mask(1)
    apply_mask(2)
    z_step(HB, 2)
    gather_wait(IN_X, 1)
    partials(IN_X, groups[0], part_gu, (0, 1))
    z_step(GU, 0)
    for slots in groups[1:]:
        partials(IN_X, slots, part_gu, (0, 1))
    z_step(HB, 3)
    gather_wait(IN_COT, 1)
    partials(IN_COT, groups[0], part_dh, (2,))
    z_step(DH, 0)
    for slots in groups[1:]:
        partials(IN_COT, slots, part_dh, (2,))
    loads[4].wait()
    gather_start(IN_SAVED, 0)
    for s in range(1, half + 1):
        z_step(GU, s)
        if s > 1:
            z_step(DH, s - 1)
        if s == 1:
            turn(0, IN_COT)
        if s == 2:
            gather_wait(IN_SAVED, 0)
            gather_start(IN_SAVED, 1)
            z_step(HB, 4)
    gather_wait(IN_SAVED, 1)
    gate_up = reduced(GU)
    gate_f, up_f = gate_up[0], gate_up[1]
    full_hf[0, 0] = (gate_f * jax.nn.sigmoid(gate_f) * up_f).astype(BF16)
    z_step(HF, 0)
    z_step(DH, half)
    dhid = reduced(DH)[0]
    gate_b, up_b = sg_v[...].astype(F32), su_v[...].astype(F32)
    sig = jax.nn.sigmoid(gate_b)
    full_dd[0, 0] = (dhid * up_b * sig * (1.0 + gate_b * (1.0 - sig))).astype(BF16)
    full_dd[0, 1] = (dhid * gate_b * sig).astype(BF16)
    z_step(DD, 0)
    z_step(HB, 5)
    turn(1, IN_SAVED)
    pending = [0]
    for s in range(1, half + 1):
        z_step(HF, s)
        z_step(DD, s)
        pending += [s, ring - s] if s < half else [s]
        if s % 2 == 0 or s >= half - 1:
            back_product(OUT_Y, pending)
            back_product(OUT_DX, pending)
            pending = []
        if s == min(4, half):
            z_step(HB, 6)
    weight_grad(1, full_dd, 0, 0, grad_gate)
    z_step(HB, 7)
    weight_grad(1, full_dd, 1, 1, grad_up)
    ffn = fold_end(OUT_Y)
    back = fold_end(OUT_DX)
    result_y = jnp.where(positions < counts[0], acts[IN_X, y, x].astype(F32) + ffn, 0.0).astype(BF16)
    result_dx = (acts[IN_COT, y, x].astype(F32) + back).astype(BF16)
    first = jnp.full((chunk, depth), pipe, jnp.int32) == 0
    message[...] = jnp.where(first, result_y.astype(F32), result_dx.astype(F32)).astype(BF16)
    leaving[...] = jnp.where(first, result_dx.astype(F32), result_y.astype(F32)).astype(BF16)
    swap = remote(message, handoff.at[0], p_send, p_recv, {"pipe": 1 - pipe})
    swap.start()
    stores.append(pltpu.make_async_copy(leaving, outward.at[0], store_sem.at[3]))
    stores[-1].start()
    z_step(HB, 8)
    weight_grad(0, full_hb, 0, 2, grad_down)
    for stream in (GU, DH, HF, DD, HB):
        z_finish(stream)
    for which in (IN_X, IN_COT, IN_SAVED):
        ref = outs.at[0, pl.ds(0, ring - 1)]
        remote(ref, ref, g_send.at[which], g_recv.at[which, 0], along_x(1)).wait_send()
    for which in (OUT_Y, OUT_DX):
        fold_all(which).wait_send()
    swap.wait()
    for store in stores:
        store.wait()


def copy_out(*refs):
    sources, targets, staged = refs[:5], refs[5:10], refs[10:15]
    load_sem, store_sem = refs[15:]
    loads, stores = [], []
    for k in (2, 3, 4, 0, 1):
        rows = sources[k].shape[1]
        pieces = 3 if rows % 48 == 0 and rows > 64 else 1
        for p in range(pieces):
            at = pl.ds(p * (rows // pieces), rows // pieces)
            n = len(loads)
            loads.append(pltpu.make_async_copy(sources[k].at[0, at], staged[k].at[at], load_sem.at[n]))
            stores.append(pltpu.make_async_copy(staged[k].at[at], targets[k].at[0, at], store_sem.at[n]))
    for load in loads:
        load.start()
    for load, store in zip(loads, stores):
        load.wait()
        store.start()
    for store in stores:
        store.wait()


def on_device(*args):
    fwd_in, saved_gate = args[0], args[2]
    _, chunk, depth = fwd_in.shape
    _, chunk_r, width = saved_gate.shape
    ring = lax.axis_size("row")
    nx = 1
    while nx * nx < ring:
        nx += 1
    assert chunk == chunk_r and ring == lax.axis_size("col") == nx * nx
    half = ring // 2
    dims = (ring, nx, chunk, depth, width)
    wide = (chunk, width)
    slim = (chunk, depth)
    blocks = (depth // BLOCK, width // BLOCK)
    hbm_spec = pl.BlockSpec(memory_space=pltpu.HBM)
    smem_spec = pl.BlockSpec(memory_space=pltpu.SMEM)
    weight = jax.ShapeDtypeStruct((1, depth, width), BF16)
    act = jax.ShapeDtypeStruct((1, chunk, depth), BF16)
    shapes = (act, act, weight, weight, weight)
    dma = pltpu.SemaphoreType.DMA
    results = pl.pallas_call(
        functools.partial(kernel, dims),
        out_shape=shapes,
        in_specs=[hbm_spec] * 11 + [smem_spec],
        out_specs=(hbm_spec,) * 5,
        scratch_shapes=[
            pltpu.VMEM((3, nx, nx) + slim, BF16),
            pltpu.VMEM(slim, BF16),
            pltpu.VMEM(wide, BF16),
            pltpu.VMEM(wide, BF16),
            pltpu.VMEM((3, depth, width), BF16),
            pltpu.VMEM((3, blocks[0], 1, blocks[1]), jnp.int32),
            pltpu.VMEM((3, 8, width), F32),
            pltpu.VMEM((ring, 2) + wide, BF16),
            pltpu.VMEM((ring, 1) + wide, BF16),
            pltpu.VMEM((ring, 1) + wide, BF16),
            pltpu.VMEM((ring, 2) + wide, BF16),
            pltpu.VMEM((ring, 1) + wide, BF16),
            pltpu.VMEM((half, 2) + wide, BF16),
            pltpu.VMEM((half - 1, 2) + wide, BF16),
            pltpu.VMEM((half, 1) + wide, BF16),
            pltpu.VMEM((half - 1, 1) + wide, BF16),
            pltpu.VMEM((2, depth, ring * chunk), BF16),
            pltpu.VMEM((2, ring) + slim, BF16),
            pltpu.VMEM((2, ring - 1) + slim, BF16),
            pltpu.VMEM(slim, BF16),
            pltpu.VMEM(slim, BF16),
            pltpu.VMEM((3, depth, width), BF16),
            dma((11,)),
            dma((5,)),
            dma((5, 2, half)),
            dma((3,)),
            dma((3, 2)),
            dma((2,)),
            dma((2,)),
            dma,
            dma,
            dma((4,)),
        ],
        compiler_params=pltpu.CompilerParams(
            collective_id=0, has_side_effects=True, vmem_limit_bytes=VMEM_LIMIT
        ),
    )(*args[:8], *(jnp.transpose(mask, (1, 0, 2)) for mask in args[8:11]), args[11])
    return pl.pallas_call(
        copy_out,
        out_shape=shapes,
        in_specs=[hbm_spec] * 5,
        out_specs=(hbm_spec,) * 5,
        scratch_shapes=[pltpu.VMEM(shape.shape[1:], BF16) for shape in shapes] + [dma((11,)), dma((11,))],
        compiler_params=pltpu.CompilerParams(vmem_limit_bytes=VMEM_LIMIT),
    )(*results)


def solution(mesh):
    tokens = P("pipe", "col", "row")
    grid = P("pipe", "row", "col")
    in_specs = (tokens, tokens, grid, grid, tokens) + (grid,) * 6 + (P(),)
    out_specs = (tokens, tokens, grid, grid, grid)
    return jax.shard_map(on_device, mesh=mesh, in_specs=in_specs, out_specs=out_specs, check_vma=False)
```

time: 116 us -> 112 us (0.966)
  the two profiles are of different devices: /device:TPU:2 before, /device:TPU:17 now
where the time goes in v3:
time: 112 us
  Pallas kernels  112 us (100%)
    pallas_call x1, Pallas kernels, on_device(): pl.pallas_call(functools.partial(kernel, dims), out_shape=shapes, in_spec...  109 us
    pallas_call x1, Pallas kernels, on_device(): pl.pallas_call(copy_out, out_shape=shapes, in_specs=[hbm_spec] * 5, out_s...  2.54 us

profile of v3, /device:TPU:17, one launch (start us, length us, event | category | flops | bytes accessed | tf_op | source)
XLA Modules:
  0.0 112.2 jit_solution(4409419359969354391)
XLA Ops:
  0.6 109.0 %shard_map.155 = (bf16[1,32,384]{2,1,0:T(8,128)(2,1)}, bf16[1,32,384]{2,1,0:T(8,128)(2,1)}, bf16[1,384,896]{2,1,0:T(8,128)(2,1)}, bf16[1,384,896]{2,1,0:T(8,128)(2,1)}, bf16[1,384,896]{2,1,0:T(8,128)(2,1)}) custom-call(bf16[1,32,384]{2,1,0:T(8,128)(2,1)} %fwd_in.1, bf16[1,32,384]{2,1,0:T(8,128)(2,1)} %saved_in.1, bf16[1,32,896]{2,1,0:T(8,128)(2,1)} %saved_gate.1, ...), custom_call_target="tpu_custom_call" | custom-call | tf_op jit(solution)/shard_map/pallas_call | solution.py:364
  109.6 2.5 %shard_map.156 = (bf16[1,32,384]{2,1,0:T(8,128)(2,1)}, bf16[1,32,384]{2,1,0:T(8,128)(2,1)}, bf16[1,384,896]{2,1,0:T(8,128)(2,1)}, bf16[1,384,896]{2,1,0:T(8,128)(2,1)}, bf16[1,384,896]{2,1,0:T(8,128)(2,1)}) custom-call(bf16[1,32,384]{2,1,0:T(8,128)(2,1)} %get-tuple-element.10.refs_0_, bf16[1,32,384]{2,1,0:T(8,128)(2,1)} %get-tuple-element.11.refs_1_, ...), custom_call_target="tpu_custom_call" | custom-call | tf_op jit(solution)/shard_map/pallas_call | solution.py:407

commit v4 on v3

--- a/solution.py
+++ b/solution.py
@@ -12,7 +12,8 @@
 F32 = jnp.float32
 MESH = pl.DeviceIdType.MESH
 VMEM_LIMIT = 63 * 1024 * 1024
-GU, DH, HF, DD, HB = range(5)
+GATE, UP, DH, HF, DG, DU, HB = range(7)
+PIECES = (2, 2, 2, 2, 2, 2, 2)
 IN_X, IN_COT, IN_SAVED = range(3)
 OUT_Y, OUT_DX = range(2)
 
@@ -24,8 +25,7 @@
     mask_gate, mask_up, mask_down, counts,
     handoff, outward, grad_gate, grad_up, grad_down,
     acts, go_v, sg_v, su_v, weights, mask_v, mask_rows,
-    part_gu, part_dh, full_hf, full_dd, full_hb,
-    land_gu_a, land_gu_b, land_dh_a, land_dh_b, turned,
+    part, land_a, land_b, full, turned,
     outs, out_land, message, leaving, stage,
     load_sem, z_send, z_recv, g_send, g_recv, f_send, f_recv,
     p_send, p_recv, store_sem,
@@ -72,47 +72,51 @@
             device_id=device, device_id_type=MESH,
         )
 
-    sums = {GU: (part_gu, land_gu_a, land_gu_b), DH: (part_dh, land_dh_a, land_dh_b)}
-    fulls = {HF: full_hf, DD: full_dd, HB: full_hb}
-
     def arms(stream):
-        longer = 1 if stream in (GU, DD) else -1
+        longer = 1 if stream % 2 == 0 else -1
         return ((longer, half), (-longer, half - 1))
 
-    def z_copy(stream, arm, step):
+    def rows_at(stream, h):
+        size = chunk // PIECES[stream]
+        return pl.ds(h * size, size)
+
+    def z_copy(stream, arm, step, h):
         d, n = arms(stream)[arm]
-        if stream in sums:
-            src = sums[stream][0].at[(d * (n - step)) % ring]
-            dst = sums[stream][1 + arm].at[step]
+        rows = rows_at(stream, h)
+        if stream <= DH:
+            src = part.at[stream, (d * (n - step)) % ring, rows]
+            dst = (land_a, land_b)[arm].at[stream, step, rows]
         else:
-            src = fulls[stream].at[(-d * step) % ring]
-            dst = fulls[stream].at[(-d * (step + 1)) % ring]
+            src = full.at[stream - HF, (-d * step) % ring, rows]
+            dst = full.at[stream - HF, (-d * (step + 1)) % ring, rows]
+        index = (ring - 1) * sum(PIECES[:stream]) + (arm * half + step) * PIECES[stream] + h
         return remote(
-            src, dst, z_send.at[stream], z_recv.at[stream, arm, step],
-            {"row": right if d == 1 else left},
+            src, dst, z_send.at[stream], z_recv.at[index], {"row": right if d == 1 else left}
         )
 
     def z_step(stream, step):
-        for arm in range(2):
-            d, n = arms(stream)[arm]
-            if 0 < step <= n:
-                z_copy(stream, arm, step - 1).wait_recv()
-                if stream in sums and step < n:
-                    part = sums[stream][0]
-                    slot = (d * (n - step)) % ring
-                    land = sums[stream][1 + arm][step - 1]
-                    part[slot] = (part[slot].astype(F32) + land.astype(F32)).astype(BF16)
-            if step < n:
-                z_copy(stream, arm, step).start()
+        for h in range(PIECES[stream]):
+            rows = rows_at(stream, h)
+            for arm in range(2):
+                d, n = arms(stream)[arm]
+                if 0 < step <= n:
+                    z_copy(stream, arm, step - 1, h).wait_recv()
+                    if stream <= DH and step < n:
+                        slot = (d * (n - step)) % ring
+                        land = (land_a, land_b)[arm][stream, step - 1, rows].astype(F32)
+                        part[stream, slot, rows] = (part[stream, slot, rows].astype(F32) + land).astype(BF16)
+                if step < n:
+                    z_copy(stream, arm, step, h).start()
 
     def z_finish(stream):
-        ref = (sums[stream][0] if stream in sums else fulls[stream]).at[pl.ds(0, ring - 1)]
-        remote(ref, ref, z_send.at[stream], z_recv.at[stream, 0, 0], {"row": right}).wait_send()
+        ref = full.at[0, pl.ds(0, ring - 1)]
+        remote(ref, ref, z_send.at[stream], z_recv.at[0], {"row": right}).wait_send()
 
     def reduced(stream):
-        part, land_a, land_b = sums[stream]
         return (
-            part[0].astype(F32) + land_a[half - 1].astype(F32) + land_b[half - 2].astype(F32)
+            part[stream, 0].astype(F32)
+            + land_a[stream, half - 1].astype(F32)
+            + land_b[stream, half - 2].astype(F32)
         )
 
     cut = chunk // 2
@@ -187,17 +191,17 @@
     first_slots = [(half - quarter // 2 + k) % ring for k in range(quarter)]
     groups = [[(j + g * quarter) % ring for j in first_slots] for g in (0, 3, 1, 2)]
 
-    def partials(which, slots, part, ks):
+    def partials(which, slots, streams):
         lhs = rows_of(which, slots)
-        for u, k in enumerate(ks):
-            product = jnp.dot(lhs, weights[k], preferred_element_type=F32).astype(BF16)
+        for stream in streams:
+            product = jnp.dot(lhs, weights[stream], preferred_element_type=F32).astype(BF16)
             for m, j in enumerate(slots):
-                part[j, u] = product[m * chunk:(m + 1) * chunk]
+                part[stream, j] = product[m * chunk:(m + 1) * chunk]
 
     def back_product(which, slots):
         total = None
-        for full, u, k in (((full_hf, 0, 2),), ((full_dd, 0, 0), (full_dd, 1, 1)))[which]:
-            lhs = jnp.concatenate([full[j, u] for j in slots], axis=0)
+        for stream, k in (((HF, 2),), ((DG, 0), (DU, 1)))[which]:
+            lhs = jnp.concatenate([full[stream - HF, j] for j in slots], axis=0)
             term = lax.dot_general(
                 lhs, weights[k], (((1,), (1,)), ((), ())), preferred_element_type=F32
             )
@@ -214,8 +218,8 @@
 
     stores = []
 
-    def weight_grad(k, full, u, index, out):
-        rhs = full[:, u].reshape(ring * chunk, width)
+    def weight_grad(k, stream, index, out):
+        rhs = full[stream - HF].reshape(ring * chunk, width)
         for i in range(depth // BLOCK):
             at = pl.ds(i * BLOCK, BLOCK)
             product = jnp.dot(turned[k, at], rhs, preferred_element_type=F32)
@@ -228,7 +232,7 @@
     loads[0].wait()
     loads[1].wait()
     gate_b, up_b = sg_v[...].astype(F32), su_v[...].astype(F32)
-    full_hb[0, 0] = (gate_b * jax.nn.sigmoid(gate_b) * up_b).astype(BF16)
+    full[HB - HF, 0] = (gate_b * jax.nn.sigmoid(gate_b) * up_b).astype(BF16)
     z_step(HB, 0)
     loads[2].wait()
     positions = col * chunk + lax.broadcasted_iota(jnp.int32, (chunk, depth), 0)
@@ -245,20 +249,22 @@
     apply_mask(2)
     z_step(HB, 2)
     gather_wait(IN_X, 1)
-    partials(IN_X, groups[0], part_gu, (0, 1))
-    z_step(GU, 0)
+    partials(IN_X, groups[0], (GATE, UP))
+    z_step(GATE, 0)
+    z_step(UP, 0)
     for slots in groups[1:]:
-        partials(IN_X, slots, part_gu, (0, 1))
+        partials(IN_X, slots, (GATE, UP))
     z_step(HB, 3)
     gather_wait(IN_COT, 1)
-    partials(IN_COT, groups[0], part_dh, (2,))
+    partials(IN_COT, groups[0], (DH,))
     z_step(DH, 0)
     for slots in groups[1:]:
-        partials(IN_COT, slots, part_dh, (2,))
+        partials(IN_COT, slots, (DH,))
     loads[4].wait()
     gather_start(IN_SAVED, 0)
     for s in range(1, half + 1):
-        z_step(GU, s)
+        z_step(GATE, s)
+        z_step(UP, s)
         if s > 1:
             z_step(DH, s - 1)
         if s == 1:
@@ -268,23 +274,24 @@
             gather_start(IN_SAVED, 1)
             z_step(HB, 4)
     gather_wait(IN_SAVED, 1)
-    gate_up = reduced(GU)
-    gate_f, up_f = gate_up[0], gate_up[1]
-    full_hf[0, 0] = (gate_f * jax.nn.sigmoid(gate_f) * up_f).astype(BF16)
+    gate_f, up_f = reduced(GATE), reduced(UP)
+    full[0, 0] = (gate_f * jax.nn.sigmoid(gate_f) * up_f).astype(BF16)
     z_step(HF, 0)
     z_step(DH, half)
-    dhid = reduced(DH)[0]
+    dhid = reduced(DH)
     gate_b, up_b = sg_v[...].astype(F32), su_v[...].astype(F32)
     sig = jax.nn.sigmoid(gate_b)
-    full_dd[0, 0] = (dhid * up_b * sig * (1.0 + gate_b * (1.0 - sig))).astype(BF16)
-    full_dd[0, 1] = (dhid * gate_b * sig).astype(BF16)
-    z_step(DD, 0)
+    full[DG - HF, 0] = (dhid * up_b * sig * (1.0 + gate_b * (1.0 - sig))).astype(BF16)
+    full[DU - HF, 0] = (dhid * gate_b * sig).astype(BF16)
+    z_step(DG, 0)
+    z_step(DU, 0)
     z_step(HB, 5)
     turn(1, IN_SAVED)
     pending = [0]
     for s in range(1, half + 1):
         z_step(HF, s)
-        z_step(DD, s)
+        z_step(DG, s)
+        z_step(DU, s)
         pending += [s, ring - s] if s < half else [s]
         if s % 2 == 0 or s >= half - 1:
             back_product(OUT_Y, pending)
@@ -292,9 +299,9 @@
             pending = []
         if s == min(4, half):
             z_step(HB, 6)
-    weight_grad(1, full_dd, 0, 0, grad_gate)
+    weight_grad(1, DG, 0, grad_gate)
     z_step(HB, 7)
-    weight_grad(1, full_dd, 1, 1, grad_up)
+    weight_grad(1, DU, 1, grad_up)
     ffn = fold_end(OUT_Y)
     back = fold_end(OUT_DX)
     result_y = jnp.where(positions < counts[0], acts[IN_X, y, x].astype(F32) + ffn, 0.0).astype(BF16)
@@ -307,8 +314,8 @@
     stores.append(pltpu.make_async_copy(leaving, outward.at[0], store_sem.at[3]))
     stores[-1].start()
     z_step(HB, 8)
-    weight_grad(0, full_hb, 0, 2, grad_down)
-    for stream in (GU, DH, HF, DD, HB):
+    weight_grad(0, HB, 2, grad_down)
+    for stream in range(7):
         z_finish(stream)
     for which in (IN_X, IN_COT, IN_SAVED):
         ref = outs.at[0, pl.ds(0, ring - 1)]
@@ -374,15 +381,10 @@
             pltpu.VMEM((3, depth, width), BF16),
             pltpu.VMEM((3, blocks[0], 1, blocks[1]), jnp.int32),
             pltpu.VMEM((3, 8, width), F32),
-            pltpu.VMEM((ring, 2) + wide, BF16),
-            pltpu.VMEM((ring, 1) + wide, BF16),
-            pltpu.VMEM((ring, 1) + wide, BF16),
-            pltpu.VMEM((ring, 2) + wide, BF16),
-            pltpu.VMEM((ring, 1) + wide, BF16),
-            pltpu.VMEM((half, 2) + wide, BF16),
-            pltpu.VMEM((half - 1, 2) + wide, BF16),
-            pltpu.VMEM((half, 1) + wide, BF16),
-            pltpu.VMEM((half - 1, 1) + wide, BF16),
+            pltpu.VMEM((3, ring) + wide, BF16),
+            pltpu.VMEM((3, half) + wide, BF16),
+            pltpu.VMEM((3, half - 1) + wide, BF16),
+            pltpu.VMEM((4, ring) + wide, BF16),
             pltpu.VMEM((2, depth, ring * chunk), BF16),
             pltpu.VMEM((2, ring) + slim, BF16),
             pltpu.VMEM((2, ring - 1) + slim, BF16),
@@ -390,8 +392,8 @@
             pltpu.VMEM(slim, BF16),
             pltpu.VMEM((3, depth, width), BF16),
             dma((11,)),
-            dma((5,)),
-            dma((5, 2, half)),
+            dma((7,)),
+            dma(((ring - 1) * sum(PIECES),)),
             dma((3,)),
             dma((3, 2)),
             dma((2,)),

time: 112 us -> 103 us (0.920)
  Pallas kernels: 112 us -> 102 us
    pallas_call x1, Pallas kernels: 109 us -> 99.3 us  [on_device(): pl.pallas_call(functools.partial(kernel, dims), out_shape=shapes, in_spec...]
where the time goes in v4:
time: 103 us; the launch traced here: 102 us
  Pallas kernels  102 us (99%)
    pallas_call x1, Pallas kernels, on_device(): pl.pallas_call(functools.partial(kernel, dims), out_shape=shapes, in_spec...  99.3 us
    pallas_call x1, Pallas kernels, on_device(): pl.pallas_call(copy_out, out_shape=shapes, in_specs=[hbm_spec] * 5, out_s...  2.54 us

profile of v4, /device:TPU:17, one launch (start us, length us, event | category | flops | bytes accessed | tf_op | source)
XLA Modules:
  0.0 102.5 jit_solution(1230013791268982157)
XLA Ops:
  0.6 99.3 %shard_map.155 = (bf16[1,32,384]{2,1,0:T(8,128)(2,1)}, bf16[1,32,384]{2,1,0:T(8,128)(2,1)}, bf16[1,384,896]{2,1,0:T(8,128)(2,1)}, bf16[1,384,896]{2,1,0:T(8,128)(2,1)}, bf16[1,384,896]{2,1,0:T(8,128)(2,1)}) custom-call(bf16[1,32,384]{2,1,0:T(8,128)(2,1)} %fwd_in.1, bf16[1,32,384]{2,1,0:T(8,128)(2,1)} %saved_in.1, bf16[1,32,896]{2,1,0:T(8,128)(2,1)} %saved_gate.1, ...), custom_call_target="tpu_custom_call" | custom-call | tf_op jit(solution)/shard_map/pallas_call | solution.py:371
  99.9 2.5 %shard_map.156 = (bf16[1,32,384]{2,1,0:T(8,128)(2,1)}, bf16[1,32,384]{2,1,0:T(8,128)(2,1)}, bf16[1,384,896]{2,1,0:T(8,128)(2,1)}, bf16[1,384,896]{2,1,0:T(8,128)(2,1)}, bf16[1,384,896]{2,1,0:T(8,128)(2,1)}) custom-call(bf16[1,32,384]{2,1,0:T(8,128)(2,1)} %get-tuple-element.10.refs_0_, bf16[1,32,384]{2,1,0:T(8,128)(2,1)} %get-tuple-element.11.refs_1_, ...), custom_call_target="tpu_custom_call" | custom-call | tf_op jit(solution)/shard_map/pallas_call | solution.py:409

commit v5 on v4

--- a/solution.py
+++ b/solution.py
@@ -11,7 +11,7 @@
 BF16 = jnp.bfloat16
 F32 = jnp.float32
 MESH = pl.DeviceIdType.MESH
-VMEM_LIMIT = 63 * 1024 * 1024
+VMEM_LIMIT = 61 * 1024 * 1024 + 900 * 1024
 GATE, UP, DH, HF, DG, DU, HB = range(7)
 PIECES = (2, 2, 2, 2, 2, 2, 2)
 IN_X, IN_COT, IN_SAVED = range(3)
@@ -26,9 +26,9 @@
     handoff, outward, grad_gate, grad_up, grad_down,
     acts, go_v, sg_v, su_v, weights, mask_v, mask_rows,
     part, land_a, land_b, full, turned,
-    outs, out_land, message, leaving, stage,
+    outs, out_land, message,
     load_sem, z_send, z_recv, g_send, g_recv, f_send, f_recv,
-    p_send, p_recv, store_sem,
+    p_send, p_recv,
 ):
     ring, nx, chunk, depth, width = dims
     half = ring // 2
@@ -89,24 +89,34 @@
         else:
             src = full.at[stream - HF, (-d * step) % ring, rows]
             dst = full.at[stream - HF, (-d * (step + 1)) % ring, rows]
-        index = (ring - 1) * sum(PIECES[:stream]) + (arm * half + step) * PIECES[stream] + h
+        shared = stream if stream <= DH else stream - HF
+        index = (ring - 1) * sum(PIECES[:shared]) + (arm * half + step) * PIECES[stream] + h
         return remote(
             src, dst, z_send.at[stream], z_recv.at[index], {"row": right if d == 1 else left}
         )
 
+    def z_piece(stream, step, h, arm):
+        rows = rows_at(stream, h)
+        d, n = arms(stream)[arm]
+        if 0 < step <= n:
+            z_copy(stream, arm, step - 1, h).wait_recv()
+            if stream <= DH and step < n:
+                slot = (d * (n - step)) % ring
+                land = (land_a, land_b)[arm][stream, step - 1, rows].astype(F32)
+                part[stream, slot, rows] = (part[stream, slot, rows].astype(F32) + land).astype(BF16)
+        if step < n:
+            z_copy(stream, arm, step, h).start()
+
+    def z_steps(*steps):
+        for h in range(2):
+            for stream, step in steps:
+                for arm in range(2):
+                    z_piece(stream, step, h, arm)
+
     def z_step(stream, step):
         for h in range(PIECES[stream]):
-            rows = rows_at(stream, h)
             for arm in range(2):
-                d, n = arms(stream)[arm]
-                if 0 < step <= n:
-                    z_copy(stream, arm, step - 1, h).wait_recv()
-                    if stream <= DH and step < n:
-                        slot = (d * (n - step)) % ring
-                        land = (land_a, land_b)[arm][stream, step - 1, rows].astype(F32)
-                        part[stream, slot, rows] = (part[stream, slot, rows].astype(F32) + land).astype(BF16)
-                if step < n:
-                    z_copy(stream, arm, step, h).start()
+                z_piece(stream, step, h, arm)
 
     def z_finish(stream):
         ref = full.at[0, pl.ds(0, ring - 1)]
@@ -216,17 +226,13 @@
             slots = range(g, g + quarter)
             turned[k, :, pl.ds(g * chunk, quarter * chunk)] = rows_of(which, slots).T
 
-    stores = []
 
     def weight_grad(k, stream, index, out):
         rhs = full[stream - HF].reshape(ring * chunk, width)
         for i in range(depth // BLOCK):
             at = pl.ds(i * BLOCK, BLOCK)
             product = jnp.dot(turned[k, at], rhs, preferred_element_type=F32)
-            stage[index, at] = (product * mask_row(index, i)).astype(BF16)
-        store = pltpu.make_async_copy(stage.at[index], out.at[0], store_sem.at[index])
-        store.start()
-        stores.append(store)
+            out[0, at] = (product * mask_row(index, i)).astype(BF16)
 
     gather_start(IN_X, 0, fwd_in.at[0])
     loads[0].wait()
@@ -255,6 +261,8 @@
     for slots in groups[1:]:
         partials(IN_X, slots, (GATE, UP))
     z_step(HB, 3)
+    z_step(GATE, 1)
+    z_step(UP, 1)
     gather_wait(IN_COT, 1)
     partials(IN_COT, groups[0], (DH,))
     z_step(DH, 0)
@@ -263,16 +271,16 @@
     loads[4].wait()
     gather_start(IN_SAVED, 0)
     for s in range(1, half + 1):
-        z_step(GATE, s)
-        z_step(UP, s)
         if s > 1:
-            z_step(DH, s - 1)
+            z_steps((GATE, s), (UP, s), (DH, s - 1))
         if s == 1:
+            z_step(HB, 4)
             turn(0, IN_COT)
+        if s == half:
+            z_step(HB, 5)
         if s == 2:
             gather_wait(IN_SAVED, 0)
             gather_start(IN_SAVED, 1)
-            z_step(HB, 4)
     gather_wait(IN_SAVED, 1)
     gate_f, up_f = reduced(GATE), reduced(UP)
     full[0, 0] = (gate_f * jax.nn.sigmoid(gate_f) * up_f).astype(BF16)
@@ -285,22 +293,19 @@
     full[DU - HF, 0] = (dhid * gate_b * sig).astype(BF16)
     z_step(DG, 0)
     z_step(DU, 0)
-    z_step(HB, 5)
+    z_step(HB, 6)
     turn(1, IN_SAVED)
     pending = [0]
     for s in range(1, half + 1):
-        z_step(HF, s)
-        z_step(DG, s)
-        z_step(DU, s)
+        z_steps((HF, s), (DG, s), (DU, s))
         pending += [s, ring - s] if s < half else [s]
         if s % 2 == 0 or s >= half - 1:
             back_product(OUT_Y, pending)
             back_product(OUT_DX, pending)
             pending = []
-        if s == min(4, half):
-            z_step(HB, 6)
+        if s == half - 1:
+            z_step(HB, 7)
     weight_grad(1, DG, 0, grad_gate)
-    z_step(HB, 7)
     weight_grad(1, DU, 1, grad_up)
     ffn = fold_end(OUT_Y)
     back = fold_end(OUT_DX)
@@ -308,11 +313,9 @@
     result_dx = (acts[IN_COT, y, x].astype(F32) + back).astype(BF16)
     first = jnp.full((chunk, depth), pipe, jnp.int32) == 0
     message[...] = jnp.where(first, result_y.astype(F32), result_dx.astype(F32)).astype(BF16)
-    leaving[...] = jnp.where(first, result_dx.astype(F32), result_y.astype(F32)).astype(BF16)
+    outward[0] = jnp.where(first, result_dx.astype(F32), result_y.astype(F32)).astype(BF16)
     swap = remote(message, handoff.at[0], p_send, p_recv, {"pipe": 1 - pipe})
     swap.start()
-    stores.append(pltpu.make_async_copy(leaving, outward.at[0], store_sem.at[3]))
-    stores[-1].start()
     z_step(HB, 8)
     weight_grad(0, HB, 2, grad_down)
     for stream in range(7):
@@ -323,29 +326,14 @@
     for which in (OUT_Y, OUT_DX):
         fold_all(which).wait_send()
     swap.wait()
-    for store in stores:
-        store.wait()
 
 
 def copy_out(*refs):
-    sources, targets, staged = refs[:5], refs[5:10], refs[10:15]
-    load_sem, store_sem = refs[15:]
-    loads, stores = [], []
-    for k in (2, 3, 4, 0, 1):
-        rows = sources[k].shape[1]
-        pieces = 3 if rows % 48 == 0 and rows > 64 else 1
-        for p in range(pieces):
-            at = pl.ds(p * (rows // pieces), rows // pieces)
-            n = len(loads)
-            loads.append(pltpu.make_async_copy(sources[k].at[0, at], staged[k].at[at], load_sem.at[n]))
-            stores.append(pltpu.make_async_copy(staged[k].at[at], targets[k].at[0, at], store_sem.at[n]))
-    for load in loads:
-        load.start()
-    for load, store in zip(loads, stores):
-        load.wait()
-        store.start()
-    for store in stores:
-        store.wait()
+    copies = [pltpu.make_async_copy(refs[k], refs[5 + k], refs[10].at[k]) for k in range(5)]
+    for copy in copies:
+        copy.start()
+    for copy in copies:
+        copy.wait()
 
 
 def on_device(*args):
@@ -363,16 +351,15 @@
     slim = (chunk, depth)
     blocks = (depth // BLOCK, width // BLOCK)
     hbm_spec = pl.BlockSpec(memory_space=pltpu.HBM)
+    vmem_spec = pl.BlockSpec(memory_space=pltpu.VMEM)
     smem_spec = pl.BlockSpec(memory_space=pltpu.SMEM)
-    weight = jax.ShapeDtypeStruct((1, depth, width), BF16)
-    act = jax.ShapeDtypeStruct((1, chunk, depth), BF16)
-    shapes = (act, act, weight, weight, weight)
+    weight_shape, act_shape = (1, depth, width), (1, chunk, depth)
     dma = pltpu.SemaphoreType.DMA
     results = pl.pallas_call(
         functools.partial(kernel, dims),
-        out_shape=shapes,
+        out_shape=(pltpu.VMEM(act_shape, BF16),) * 2 + (pltpu.VMEM(weight_shape, BF16),) * 3,
         in_specs=[hbm_spec] * 11 + [smem_spec],
-        out_specs=(hbm_spec,) * 5,
+        out_specs=(vmem_spec,) * 5,
         scratch_shapes=[
             pltpu.VMEM((3, nx, nx) + slim, BF16),
             pltpu.VMEM(slim, BF16),
@@ -389,30 +376,28 @@
             pltpu.VMEM((2, ring) + slim, BF16),
             pltpu.VMEM((2, ring - 1) + slim, BF16),
             pltpu.VMEM(slim, BF16),
-            pltpu.VMEM(slim, BF16),
-            pltpu.VMEM((3, depth, width), BF16),
             dma((11,)),
             dma((7,)),
-            dma(((ring - 1) * sum(PIECES),)),
+            dma(((ring - 1) * sum(PIECES[HF:]),)),
             dma((3,)),
             dma((3, 2)),
             dma((2,)),
             dma((2,)),
             dma,
             dma,
-            dma((4,)),
         ],
         compiler_params=pltpu.CompilerParams(
             collective_id=0, has_side_effects=True, vmem_limit_bytes=VMEM_LIMIT
         ),
     )(*args[:8], *(jnp.transpose(mask, (1, 0, 2)) for mask in args[8:11]), args[11])
+
     return pl.pallas_call(
         copy_out,
-        out_shape=shapes,
-        in_specs=[hbm_spec] * 5,
+        out_shape=tuple(jax.ShapeDtypeStruct(result.shape, BF16) for result in results),
+        in_specs=[pl.BlockSpec(memory_space=pl.ANY)] * 5,
         out_specs=(hbm_spec,) * 5,
-        scratch_shapes=[pltpu.VMEM(shape.shape[1:], BF16) for shape in shapes] + [dma((11,)), dma((11,))],
-        compiler_params=pltpu.CompilerParams(vmem_limit_bytes=VMEM_LIMIT),
+        scratch_shapes=[dma((5,))],
+        compiler_params=pltpu.CompilerParams(vmem_limit_bytes=8 * 1024 * 1024),
     )(*results)
 
 

time: 103 us -> 101 us (0.981)
  Pallas kernels: 102 us -> 99.9 us
    pallas_call x2, Pallas kernels: 102 us -> 99.9 us  [the longest x1 98.5 us: on_device(): pl.pallas_call(functools.partial(kernel, dims), out_shape=(pltpu.VMEM(act...]
where the time goes in v5:
time: 101 us
  Pallas kernels  99.9 us (99%)
    pallas_call x1, Pallas kernels, on_device(): pl.pallas_call(functools.partial(kernel, dims), out_shape=(pltpu.VMEM(act...  98.5 us

profile of v5, /device:TPU:17, one launch (start us, length us, event | category | flops | bytes accessed | tf_op | source)
XLA Modules:
  0.0 100.5 jit_solution(3595652913418796563)
XLA Ops:
  0.6 98.5 %shard_map.155 = (bf16[1,32,384]{2,1,0:T(8,128)(2,1)S(1)}, bf16[1,32,384]{2,1,0:T(8,128)(2,1)S(1)}, bf16[1,384,896]{2,1,0:T(8,128)(2,1)S(1)}, bf16[1,384,896]{2,1,0:T(8,128)(2,1)S(1)}, bf16[1,384,896]{2,1,0:T(8,128)(2,1)S(1)}) custom-call(bf16[1,32,384]{2,1,0:T(8,128)(2,1)} %fwd_in.1, bf16[1,32,384]{2,1,0:T(8,128)(2,1)} %saved_in.1, ...), custom_call_target="tpu_custom_call" | custom-call | tf_op jit(solution)/shard_map/pallas_call | solution.py:358
  99.1 1.4 %shard_map.156 = (bf16[1,32,384]{2,1,0:T(8,128)(2,1)}, bf16[1,32,384]{2,1,0:T(8,128)(2,1)}, bf16[1,384,896]{2,1,0:T(8,128)(2,1)}, bf16[1,384,896]{2,1,0:T(8,128)(2,1)}, bf16[1,384,896]{2,1,0:T(8,128)(2,1)}) custom-call(bf16[1,32,384]{2,1,0:T(8,128)(2,1)S(1)} %get-tuple-element.10.refs_0_, bf16[1,32,384]{2,1,0:T(8,128)(2,1)S(1)} %get-tuple-element.11.refs_1_, ...), custom_call_target="tpu_custom_call" | custom-call | tf_op jit(solution)/shard_map/pallas_call | solution.py:394

commit v6 on v5

--- a/solution.py
+++ b/solution.py
@@ -8,6 +8,7 @@
 from jax.sharding import PartitionSpec as P
 
 BLOCK = 128
+LEAD = 2
 BF16 = jnp.bfloat16
 F32 = jnp.float32
 MESH = pl.DeviceIdType.MESH
@@ -28,7 +29,7 @@
     part, land_a, land_b, full, turned,
     outs, out_land, message,
     load_sem, z_send, z_recv, g_send, g_recv, f_send, f_recv,
-    p_send, p_recv,
+    p_send, p_recv, pace,
 ):
     ring, nx, chunk, depth, width = dims
     half = ring // 2
@@ -90,7 +91,7 @@
             src = full.at[stream - HF, (-d * step) % ring, rows]
             dst = full.at[stream - HF, (-d * (step + 1)) % ring, rows]
         shared = stream if stream <= DH else stream - HF
-        index = (ring - 1) * sum(PIECES[:shared]) + (arm * half + step) * PIECES[stream] + h
+        index = (shared * 2 + arm) * 4 * 2 + (step % 4) * 2 + h
         return remote(
             src, dst, z_send.at[stream], z_recv.at[index], {"row": right if d == 1 else left}
         )
@@ -115,6 +116,11 @@
 
     def z_step(stream, step):
         for h in range(PIECES[stream]):
+            for arm in range(2):
+                z_piece(stream, step, h, arm)
+
+    def z_part(*pieces):
+        for stream, step, h in pieces:
             for arm in range(2):
                 z_piece(stream, step, h, arm)
 
@@ -233,6 +239,18 @@
             at = pl.ds(i * BLOCK, BLOCK)
             product = jnp.dot(turned[k, at], rhs, preferred_element_type=F32)
             out[0, at] = (product * mask_row(index, i)).astype(BF16)
+
+    def round_start(number):
+        if number > LEAD:
+            @pl.when(pipe == 1)
+            def _():
+                pl.semaphore_wait(pace, 1)
+
+    def round_end(number):
+        if number <= 2 * half - LEAD:
+            @pl.when(pipe == 0)
+            def _():
+                pl.semaphore_signal(pace, inc=1, device_id={"pipe": 1 - pipe}, device_id_type=MESH)
 
     gather_start(IN_X, 0, fwd_in.at[0])
     loads[0].wait()
@@ -256,26 +274,27 @@
     z_step(HB, 2)
     gather_wait(IN_X, 1)
     partials(IN_X, groups[0], (GATE, UP))
-    z_step(GATE, 0)
-    z_step(UP, 0)
+    z_part((GATE, 0, 0), (GATE, 0, 1), (UP, 0, 0))
     for slots in groups[1:]:
         partials(IN_X, slots, (GATE, UP))
+    z_part((UP, 0, 1))
     z_step(HB, 3)
-    z_step(GATE, 1)
-    z_step(UP, 1)
+    z_part((GATE, 1, 0), (GATE, 1, 1), (UP, 1, 0))
     gather_wait(IN_COT, 1)
-    partials(IN_COT, groups[0], (DH,))
-    z_step(DH, 0)
-    for slots in groups[1:]:
+    for slots in groups:
         partials(IN_COT, slots, (DH,))
     loads[4].wait()
     gather_start(IN_SAVED, 0)
+    turn(0, IN_COT)
+    z_part((UP, 1, 1), (DH, 0, 0), (DH, 0, 1))
     for s in range(1, half + 1):
+        round_start(s)
         if s > 1:
-            z_steps((GATE, s), (UP, s), (DH, s - 1))
+            z_part((GATE, s, 0), (GATE, s, 1), (UP, s, 0))
+            z_part((UP, s, 1), (DH, s - 1, 0), (DH, s - 1, 1))
+        round_end(s)
         if s == 1:
             z_step(HB, 4)
-            turn(0, IN_COT)
         if s == half:
             z_step(HB, 5)
         if s == 2:
@@ -297,7 +316,11 @@
     turn(1, IN_SAVED)
     pending = [0]
     for s in range(1, half + 1):
-        z_steps((HF, s), (DG, s), (DU, s))
+        round_start(half + s)
+        z_step(HF, s)
+        z_step(DG, s)
+        z_step(DU, s)
+        round_end(half + s)
         pending += [s, ring - s] if s < half else [s]
         if s % 2 == 0 or s >= half - 1:
             back_product(OUT_Y, pending)
@@ -378,13 +401,14 @@
             pltpu.VMEM(slim, BF16),
             dma((11,)),
             dma((7,)),
-            dma(((ring - 1) * sum(PIECES[HF:]),)),
+            dma((4 * 2 * 4 * 2,)),
             dma((3,)),
             dma((3, 2)),
             dma((2,)),
             dma((2,)),
             dma,
             dma,
+            pltpu.SemaphoreType.REGULAR,
         ],
         compiler_params=pltpu.CompilerParams(
             collective_id=0, has_side_effects=True, vmem_limit_bytes=VMEM_LIMIT

time: 101 us -> 98.9 us (0.979)
  Pallas kernels: 99.9 us -> 98.1 us
    pallas_call x1, Pallas kernels: 98.5 us -> 96.7 us  [on_device(): pl.pallas_call(functools.partial(kernel, dims), out_shape=(pltpu.VMEM(act...]
where the time goes in v6:
time: 98.9 us; the launch traced here: 98.7 us
  Pallas kernels  98.1 us (99%)
    pallas_call x1, Pallas kernels, on_device(): pl.pallas_call(functools.partial(kernel, dims), out_shape=(pltpu.VMEM(act...  96.7 us

profile of v6, /device:TPU:17, one launch (start us, length us, event | category | flops | bytes accessed | tf_op | source)
XLA Modules:
  0.0 98.7 jit_solution(15687964842386788270)
XLA Ops:
  0.6 96.7 %shard_map.155 = (bf16[1,32,384]{2,1,0:T(8,128)(2,1)S(1)}, bf16[1,32,384]{2,1,0:T(8,128)(2,1)S(1)}, bf16[1,384,896]{2,1,0:T(8,128)(2,1)S(1)}, bf16[1,384,896]{2,1,0:T(8,128)(2,1)S(1)}, bf16[1,384,896]{2,1,0:T(8,128)(2,1)S(1)}) custom-call(bf16[1,32,384]{2,1,0:T(8,128)(2,1)} %fwd_in.1, bf16[1,32,384]{2,1,0:T(8,128)(2,1)} %saved_in.1, ...), custom_call_target="tpu_custom_call" | custom-call | tf_op jit(solution)/shard_map/pallas_call | solution.py:381
  97.4 1.4 %shard_map.156 = (bf16[1,32,384]{2,1,0:T(8,128)(2,1)}, bf16[1,32,384]{2,1,0:T(8,128)(2,1)}, bf16[1,384,896]{2,1,0:T(8,128)(2,1)}, bf16[1,384,896]{2,1,0:T(8,128)(2,1)}, bf16[1,384,896]{2,1,0:T(8,128)(2,1)}) custom-call(bf16[1,32,384]{2,1,0:T(8,128)(2,1)S(1)} %get-tuple-element.10.refs_0_, bf16[1,32,384]{2,1,0:T(8,128)(2,1)S(1)} %get-tuple-element.11.refs_1_, ...), custom_call_target="tpu_custom_call" | custom-call | tf_op jit(solution)/shard_map/pallas_call | solution.py:418
